TPU v7x, 512 devices: a whole 4x4x16 slice. The times are simulated.
512 devices in a mesh: blk: 32 (over x, y, core), smp: 16 (over z).
Axes of the slice: x: 4, y: 4, z: 16, core: 2. Of those that a mesh axis runs over, the one named last changes fastest.
Arguments:
- features: bfloat16 [16, 96, 8192], P('smp', None, 'blk'), may hold values from -6 to 6
- active: int32 [16, 8192], P('smp', 'blk'), may hold values 0 or 1
- neighbour_rows: int32 [16, 27, 8192], P('smp', None, 'blk'), may hold values from 0 to 400, as said below
- send_rows: int32 [16, 32, 8, 32], P('smp', 'blk'), may hold values from 0 to 256, as said below
- first_weight: bfloat16 [27, 96, 96], replicated, may hold values from -0.125 to 0.125
- second_weight: bfloat16 [27, 96, 96], replicated, may hold values from -0.125 to 0.125
- cotangent: bfloat16 [16, 96, 8192], P('smp', None, 'blk'), may hold values from -6 to 6
Outputs:
- out_field: bfloat16 [16, 96, 8192], P('smp', None, 'blk')
- input_grad: bfloat16 [16, 96, 8192], P('smp', None, 'blk')
- first_grad: float32 [27, 96, 96], replicated
- second_grad: float32 [27, 96, 96], replicated
Inputs may be any that keep to these rules, and one draw needn't show every extreme that they name: `neighbour_rows`: offset o = 9 (a + 1) + 3 (b + 1) + (c + 1) for a step (a, b, c) in -1..1 along the three dimensions; o = 13 names the voxel itself. The relation is symmetric: if v = nbr(u, o) then u = nbr(v, 26 - o). A value naming list d, place s occurs only where send_rows[t, p, d, s] is a row. send_rows[t, p, d] lists distinct rows of device p in rising order, then the filler 256; lists of directions 4 to 7 hold at most 4 rows; in every draw some list of a direction below 4 has 32 rows and some list of a direction from 4 has 4 rows.
All inputs are finite; a program needn't handle non-finite values. No bound on the sum of `active` on one device may be relied on, other than what follows from the above.
Results may differ from a plain program's by a relative error of at most 0.005.
Values may be sent and summed in bfloat16 or wider, within the bound.
A program may use at most 64 MiB of HBM per device.

v0:
```python
import jax
import jax.numpy as jnp
from jax import lax
from jax.sharding import PartitionSpec as P

BE = 4
TALL = 4


STEPS = ((-1, 0), (1, 0), (0, -1), (0, 1), (-1, -1), (-1, 1), (1, -1), (1, 1))


def from_behind(shard, axis, by):
    length = lax.axis_size(axis)
    pairs = [(i, i + by) for i in range(length) if 0 <= i + by < length]
    return lax.ppermute(shard, axis, pairs)


def step_delta(direction):
    return STEPS[direction][0] * TALL + STEPS[direction][1]


def gather_columns(extended, lookup):
    return jax.vmap(lambda portion, indices: portion[:, indices])(extended, lookup)


def share(values_in, send_lists):
    samples_here, channels, voxels = values_in.shape
    per_list = send_lists.shape[2]
    padded = jnp.concatenate(
        [values_in, jnp.zeros((samples_here, channels, 1), values_in.dtype)], axis=2
    )
    packed = gather_columns(padded, send_lists.reshape(samples_here, 8 * per_list))
    packed = packed.reshape(samples_here, channels, 8, per_list)
    faces = [None, None, None, None]
    corners = [None, None, None, None]
    for direction in range(4):
        faces[direction] = from_behind(packed[:, :, direction], "blk", step_delta(direction))
    for direction in range(4, 8):
        corners[direction - 4] = from_behind(
            packed[:, :, direction, :BE], "blk", step_delta(direction)
        )
    filler = jnp.zeros((samples_here, channels, 1), values_in.dtype)
    return jnp.concatenate([values_in] + faces + corners + [filler], axis=2)


def convolve(extended, row_table, weights):
    samples_here, channels, voxels = (extended.shape[0], weights.shape[1], row_table.shape[2])
    by_stratum = row_table.reshape(samples_here, 3, 9 * voxels)
    stacked = weights.reshape(3, 9, channels, channels)

    def convolve_accumulate(stratum, running):
        lookup = lax.dynamic_index_in_dim(by_stratum, stratum, 1, keepdims=False)
        picked = gather_columns(extended, lookup).reshape(samples_here, channels, 9, voxels)
        matrices = lax.dynamic_index_in_dim(stacked, stratum, 0, keepdims=False)
        return running + jnp.einsum(
            "oik,skov->siv", matrices, picked, preferred_element_type=jnp.float32
        )

    return lax.fori_loop(
        0, 3, convolve_accumulate, jnp.zeros((samples_here, channels, voxels), jnp.float32)
    )


def correlate(gradient, extended, row_table):
    samples_here, channels, voxels = gradient.shape
    by_stratum = row_table.reshape(samples_here, 3, 9 * voxels)

    def correlate_accumulate(stratum, running):
        lookup = lax.dynamic_index_in_dim(by_stratum, stratum, 1, keepdims=False)
        picked = gather_columns(extended, lookup).reshape(samples_here, channels, 9, voxels)
        product = jnp.einsum("siv,skov->oik", gradient, picked, preferred_element_type=jnp.float32)
        return lax.dynamic_update_index_in_dim(running, product, stratum, 0)

    summed = lax.fori_loop(
        0, 3, correlate_accumulate, jnp.zeros((3, 9, channels, channels), jnp.float32)
    )
    return summed.reshape(27, channels, channels)


def body(features, active, neighbour_rows, send_rows, first_weight, second_weight, cotangent):
    samples_here, channels, voxels = features.shape
    send_lists = send_rows[:, 0]
    live_mask = active.astype(jnp.float32)[:, None, :]
    live_sites = live_mask > 0
    first_flipped = jnp.flip(first_weight, 0).transpose(0, 2, 1)
    second_flipped = jnp.flip(second_weight, 0).transpose(0, 2, 1)
    all_slots = lax.axis_size("smp") * samples_here * lax.axis_size("blk") * voxels
    grad_scale = 1.0 / all_slots**0.5
    masked = jnp.where(live_sites, features, jnp.zeros_like(features))
    masked_ext = share(masked, send_lists)
    pre_first = live_mask * convolve(masked_ext, neighbour_rows, first_weight)
    sigmoid_pre = jax.nn.sigmoid(pre_first)
    hidden = (live_mask * (pre_first * sigmoid_pre)).astype(jnp.bfloat16)
    hidden_ext = share(hidden, send_lists)
    out_field = (live_mask * convolve(hidden_ext, neighbour_rows, second_weight)).astype(
        jnp.bfloat16
    )
    grad_out = jnp.where(live_sites, cotangent, jnp.zeros_like(cotangent))
    second_grad = correlate(grad_out, hidden_ext, neighbour_rows) * grad_scale
    grad_hidden = live_mask * convolve(share(grad_out, send_lists), neighbour_rows, second_flipped)
    grad_pre = (grad_hidden * sigmoid_pre * (1.0 + pre_first * (1.0 - sigmoid_pre))).astype(
        jnp.bfloat16
    )
    first_grad = correlate(grad_pre, masked_ext, neighbour_rows) * grad_scale
    input_sums = convolve(share(grad_pre, send_lists), neighbour_rows, first_flipped)
    input_grad = (live_mask * input_sums).astype(jnp.bfloat16)
    first_grad, second_grad = lax.psum((first_grad, second_grad), ("blk", "smp"))
    return (out_field, input_grad, first_grad, second_grad)


def solution(mesh):
    return jax.shard_map(
        body,
        mesh=mesh,
        in_specs=(
            P("smp", None, "blk"),
            P("smp", "blk"),
            P("smp", None, "blk"),
            P("smp", "blk", None, None),
            P(),
            P(),
            P("smp", None, "blk"),
        ),
        out_specs=(P("smp", None, "blk"), P("smp", None, "blk"), P(), P()),
        check_vma=False,
    )
```

profile of v0, /device:TPU:1, one launch (start us, length us, event | category | flops | bytes accessed | tf_op | source)
XLA Modules:
  0.0 778.1 jit_solution(8710151017060632112)
XLA Ops:
  72.5 28.1 %while.84 = (s32[]{:T(128)}, f32[1,96,256]{2,1,0:T(8,128)S(1)}, s32[1,3,2304]{2,1,0:T(4,128)S(1)}, bf16[1,96,401]{1,2,0:T(8,128)(2,1)S(1)}, bf16[3,9,96,96]{3,2,1,0:T(8,128)(2,1)S(1)}, /*index=5*/s32[]{:T(128)}, s32[]{:T(128)}) while((s32[]{:T(128)}, f32[1,96,256]{2,1,0:T(8,128)S(1)}, s32[1,3,2304]{2,1,0:T(4,128)S(1)}, ...), condition=%wide.region_1.2_spmd.clone, body=%wide.region_0.1_spmd.clone.sunk | while | flops 42534912 | bytes 1984615 | solution.py:60
  72.6 8.9 %gather_fusion.2 = bf16[2304,96]{1,0:T(8,128)(2,1)S(1)} fusion(bf16[1,96,401]{1,2,0:T(8,128)(2,1)S(1)} %get-tuple-element.998, s32[2304]{0:T(1024)S(1)} %fusion.87), kind=kCustom, calls=%fused_computation.clone.clone.1 | custom fusion | bytes 903168 | tf_op jit(solution)/shard_map/while/body/eval_jaxpr/vmap()/gather | solution.py:24
  82.0 8.9 %gather_fusion.2 = bf16[2304,96]{1,0:T(8,128)(2,1)S(1)} fusion(bf16[1,96,401]{1,2,0:T(8,128)(2,1)S(1)} %get-tuple-element.998, s32[2304]{0:T(1024)S(1)} %fusion.87), kind=kCustom, calls=%fused_computation.clone.clone.1 | custom fusion | bytes 903168 | tf_op jit(solution)/shard_map/while/body/eval_jaxpr/vmap()/gather | solution.py:24
  91.4 8.9 %gather_fusion.2 = bf16[2304,96]{1,0:T(8,128)(2,1)S(1)} fusion(bf16[1,96,401]{1,2,0:T(8,128)(2,1)S(1)} %get-tuple-element.998, s32[2304]{0:T(1024)S(1)} %fusion.87), kind=kCustom, calls=%fused_computation.clone.clone.1 | custom fusion | bytes 903168 | tf_op jit(solution)/shard_map/while/body/eval_jaxpr/vmap()/gather | solution.py:24
  100.9 28.1 %while.86 = (s32[]{:T(128)}, f32[1,96,256]{2,1,0:T(8,128)S(1)}, s32[1,3,2304]{2,1,0:T(4,128)S(1)}, bf16[1,96,401]{1,2,0:T(8,128)(2,1)S(1)}, bf16[3,9,96,96]{3,2,1,0:T(8,128)(2,1)S(1)}, /*index=5*/s32[]{:T(128)}, s32[]{:T(128)}) while((s32[]{:T(128)}, f32[1,96,256]{2,1,0:T(8,128)S(1)}, s32[1,3,2304]{2,1,0:T(4,128)S(1)}, ...), condition=%wide.region_5.6_spmd.clone, body=%wide.region_4.5_spmd.clone.sunk | while | flops 42534912 | bytes 1984615 | solution.py:60
  101.0 8.9 %gather_fusion.4 = bf16[2304,96]{1,0:T(8,128)(2,1)S(1)} fusion(bf16[1,96,401]{1,2,0:T(8,128)(2,1)S(1)} %get-tuple-element.977, s32[2304]{0:T(1024)S(1)} %fusion.95), kind=kCustom, calls=%fused_computation.2.clone.clone.1 | custom fusion | bytes 903168 | tf_op jit(solution)/shard_map/while/body/eval_jaxpr/vmap()/gather | solution.py:24
  110.4 8.9 %gather_fusion.4 = bf16[2304,96]{1,0:T(8,128)(2,1)S(1)} fusion(bf16[1,96,401]{1,2,0:T(8,128)(2,1)S(1)} %get-tuple-element.977, s32[2304]{0:T(1024)S(1)} %fusion.95), kind=kCustom, calls=%fused_computation.2.clone.clone.1 | custom fusion | bytes 903168 | tf_op jit(solution)/shard_map/while/body/eval_jaxpr/vmap()/gather | solution.py:24
  119.8 8.9 %gather_fusion.4 = bf16[2304,96]{1,0:T(8,128)(2,1)S(1)} fusion(bf16[1,96,401]{1,2,0:T(8,128)(2,1)S(1)} %get-tuple-element.977, s32[2304]{0:T(1024)S(1)} %fusion.95), kind=kCustom, calls=%fused_computation.2.clone.clone.1 | custom fusion | bytes 903168 | tf_op jit(solution)/shard_map/while/body/eval_jaxpr/vmap()/gather | solution.py:24
  148.1 28.1 %while.82 = (s32[]{:T(128)}, f32[3,9,96,96]{2,3,1,0:T(8,128)S(1)}, s32[1,3,2304]{2,1,0:T(4,128)S(1)}, bf16[1,96,401]{1,2,0:T(8,128)(2,1)S(1)}, bf16[1,96,256]{2,1,0:T(8,128)(2,1)S(1)}, /*index=5*/s32[]{:T(128)}) while((s32[]{:T(128)}, f32[3,9,96,96]{2,3,1,0:T(8,128)S(1)}, s32[1,3,2304]{2,1,0:T(4,128)S(1)}, bf16[1,96,401]{1,2,0:T(8,128)(2,1)S(1)}, ...), condition=%wide.region_9.10_spmd, body=%wide.region_8.9_spmd.sunk | while | flops 42485760 | bytes 2058325 | solution.py:75
  148.2 8.9 %gather_fusion = bf16[2304,96]{1,0:T(8,128)(2,1)S(1)} fusion(bf16[1,96,401]{1,2,0:T(8,128)(2,1)S(1)} %get-tuple-element.1059, s32[2304]{0:T(1024)S(1)} %fusion.79), kind=kCustom, calls=%fused_computation.4.clone.1 | custom fusion | bytes 903168 | tf_op jit(solution)/shard_map/while/body/eval_jaxpr/vmap()/gather | solution.py:24
  157.6 8.9 %gather_fusion = bf16[2304,96]{1,0:T(8,128)(2,1)S(1)} fusion(bf16[1,96,401]{1,2,0:T(8,128)(2,1)S(1)} %get-tuple-element.1059, s32[2304]{0:T(1024)S(1)} %fusion.79), kind=kCustom, calls=%fused_computation.4.clone.1 | custom fusion | bytes 903168 | tf_op jit(solution)/shard_map/while/body/eval_jaxpr/vmap()/gather | solution.py:24
  166.9 8.9 %gather_fusion = bf16[2304,96]{1,0:T(8,128)(2,1)S(1)} fusion(bf16[1,96,401]{1,2,0:T(8,128)(2,1)S(1)} %get-tuple-element.1059, s32[2304]{0:T(1024)S(1)} %fusion.79), kind=kCustom, calls=%fused_computation.4.clone.1 | custom fusion | bytes 903168 | tf_op jit(solution)/shard_map/while/body/eval_jaxpr/vmap()/gather | solution.py:24
  205.5 28.1 %while.83 = (s32[]{:T(128)}, f32[3,9,96,96]{2,3,1,0:T(8,128)S(1)}, s32[1,3,2304]{2,1,0:T(4,128)S(1)}, bf16[1,96,401]{1,2,0:T(8,128)(2,1)S(1)}, bf16[1,96,256]{2,1,0:T(8,128)(2,1)S(1)}, /*index=5*/s32[]{:T(128)}) while((s32[]{:T(128)}, f32[3,9,96,96]{2,3,1,0:T(8,128)S(1)}, s32[1,3,2304]{2,1,0:T(4,128)S(1)}, ...), condition=%wide.region_12.13_spmd, body=%wide.region_11.12_spmd.sunk | while | flops 42485760 | bytes 2058325 | solution.py:75
  215.0 8.9 %gather_fusion.1 = bf16[2304,96]{1,0:T(8,128)(2,1)S(1)} fusion(bf16[1,96,401]{1,2,0:T(8,128)(2,1)S(1)} %get-tuple-element.1077, s32[2304]{0:T(1024)S(1)} %fusion.83), kind=kCustom, calls=%fused_computation.5.clone.1 | custom fusion | bytes 903168 | tf_op jit(solution)/shard_map/while/body/eval_jaxpr/vmap()/gather | solution.py:24
  224.3 8.9 %gather_fusion.1 = bf16[2304,96]{1,0:T(8,128)(2,1)S(1)} fusion(bf16[1,96,401]{1,2,0:T(8,128)(2,1)S(1)} %get-tuple-element.1077, s32[2304]{0:T(1024)S(1)} %fusion.83), kind=kCustom, calls=%fused_computation.5.clone.1 | custom fusion | bytes 903168 | tf_op jit(solution)/shard_map/while/body/eval_jaxpr/vmap()/gather | solution.py:24
  233.6 30.9 %while.85 = (s32[]{:T(128)}, f32[1,96,256]{2,1,0:T(8,128)S(1)}, s32[1,3,2304]{2,1,0:T(4,128)S(1)}, bf16[1,96,401]{1,2,0:T(8,128)(2,1)S(1)}, bf16[3,9,96,96]{3,2,1,0:T(8,128)(2,1)}, /*index=5*/s32[]{:T(128)}, s32[]{:T(128)}) while((s32[]{:T(128)}, f32[1,96,256]{2,1,0:T(8,128)S(1)}, s32[1,3,2304]{2,1,0:T(4,128)S(1)}, ...), condition=%wide.region_3.4_spmd.clone, body=%wide.region_2.3_spmd.clone.sunk | while | flops 42534912 | bytes 1837159 | solution.py:60
  233.7 8.9 %gather_fusion.3 = bf16[2304,96]{1,0:T(8,128)(2,1)S(1)} fusion(bf16[1,96,401]{1,2,0:T(8,128)(2,1)S(1)} %get-tuple-element.1040, s32[2304]{0:T(1024)S(1)} %fusion.91), kind=kCustom, calls=%fused_computation.1.clone.clone.1 | custom fusion | bytes 903168 | tf_op jit(solution)/shard_map/while/body/eval_jaxpr/vmap()/gather | solution.py:24
  244.1 8.9 %gather_fusion.3 = bf16[2304,96]{1,0:T(8,128)(2,1)S(1)} fusion(bf16[1,96,401]{1,2,0:T(8,128)(2,1)S(1)} %get-tuple-element.1040, s32[2304]{0:T(1024)S(1)} %fusion.91), kind=kCustom, calls=%fused_computation.1.clone.clone.1 | custom fusion | bytes 903168 | tf_op jit(solution)/shard_map/while/body/eval_jaxpr/vmap()/gather | solution.py:24
  254.4 8.9 %gather_fusion.3 = bf16[2304,96]{1,0:T(8,128)(2,1)S(1)} fusion(bf16[1,96,401]{1,2,0:T(8,128)(2,1)S(1)} %get-tuple-element.1040, s32[2304]{0:T(1024)S(1)} %fusion.91), kind=kCustom, calls=%fused_computation.1.clone.clone.1 | custom fusion | bytes 903168 | tf_op jit(solution)/shard_map/while/body/eval_jaxpr/vmap()/gather | solution.py:24
  281.5 30.9 %while.87 = (s32[]{:T(128)}, f32[1,96,256]{2,1,0:T(8,128)S(1)}, s32[1,3,2304]{2,1,0:T(4,128)S(1)}, bf16[1,96,401]{1,2,0:T(8,128)(2,1)S(1)}, bf16[3,9,96,96]{3,2,1,0:T(8,128)(2,1)}, /*index=5*/s32[]{:T(128)}, s32[]{:T(128)}) while((s32[]{:T(128)}, f32[1,96,256]{2,1,0:T(8,128)S(1)}, s32[1,3,2304]{2,1,0:T(4,128)S(1)}, ...), condition=%wide.region_7.8_spmd.clone, body=%wide.region_6.7_spmd.clone.sunk | while | flops 42534912 | bytes 1837159 | solution.py:60
  281.6 8.9 %gather_fusion.5 = bf16[2304,96]{1,0:T(8,128)(2,1)S(1)} fusion(bf16[1,96,401]{1,2,0:T(8,128)(2,1)S(1)} %get-tuple-element.1019, s32[2304]{0:T(1024)S(1)} %fusion.99), kind=kCustom, calls=%fused_computation.3.clone.clone.1 | custom fusion | bytes 903168 | tf_op jit(solution)/shard_map/while/body/eval_jaxpr/vmap()/gather | solution.py:24
  291.9 8.9 %gather_fusion.5 = bf16[2304,96]{1,0:T(8,128)(2,1)S(1)} fusion(bf16[1,96,401]{1,2,0:T(8,128)(2,1)S(1)} %get-tuple-element.1019, s32[2304]{0:T(1024)S(1)} %fusion.99), kind=kCustom, calls=%fused_computation.3.clone.clone.1 | custom fusion | bytes 903168 | tf_op jit(solution)/shard_map/while/body/eval_jaxpr/vmap()/gather | solution.py:24
  302.2 8.9 %gather_fusion.5 = bf16[2304,96]{1,0:T(8,128)(2,1)S(1)} fusion(bf16[1,96,401]{1,2,0:T(8,128)(2,1)S(1)} %get-tuple-element.1019, s32[2304]{0:T(1024)S(1)} %fusion.99), kind=kCustom, calls=%fused_computation.3.clone.clone.1 | custom fusion | bytes 903168 | tf_op jit(solution)/shard_map/while/body/eval_jaxpr/vmap()/gather | solution.py:24
  314.2 453.4 %all-reduce.7.cloned.1.call-done = (f32[27,96,96]{2,1,0:T(8,128)}, f32[27,96,96]{2,1,0:T(8,128)}) async-done(((f32[27,96,96]{2,1,0:T(8,128)}, f32[27,96,96]{2,1,0:T(8,128)}), (f32[27,96,96]{2,1,0:T(8,128)}, f32[27,96,96]{2,1,0:T(8,128)})) %all-reduce.7.cloned.1.call-update) | async-done | bytes 1990672 | tf_op jit(solution)/shard_map/psum | solution.py:108
  (211 shorter events, 157.5 us)
Async XLA Ops:
  7.2 760.5 %all-reduce.7.cloned.1.call-start = ((), (), s32[]{:S(2)}) async-start(), calls=%async_computation | async-start | bytes 5308416 | tf_op jit(solution)/shard_map/psum | solution.py:108
  18.3 17.1 %collective-permute-start.6 = (bf16[1,96,4]{1,2,0:T(4,128)(2,1)S(1)}, bf16[1,96,4]{1,2,0:T(4,128)(2,1)S(1)}, u32[]{:S(2)}, u32[]{:S(2)}) collective-permute-start(bf16[1,96,4]{1,2,0:T(4,128)(2,1)S(1)} %get-tuple-element.763), channel_id=1, source_target_pairs={{0,48},{16,64},{32,80},{48,96},{64,112},{80,128},{96,144},{112,160... | collective-permute-start | bytes 2312 | tf_op jit(solution)/shard_map/ppermute | solution.py:16
  22.4 28.3 %collective-permute-start.3 = (bf16[1,96,32]{1,2,0:T(8,128)(2,1)S(1)}, bf16[1,96,32]{1,2,0:T(8,128)(2,1)S(1)}, u32[]{:S(2)}, u32[]{:S(2)}) collective-permute-start(bf16[1,96,32]{1,2,0:T(8,128)(2,1)S(1)} %get-tuple-element.766), channel_id=1, source_target_pairs={{0,16},{16,32},{32,48},{48,64},{64,80},{80,96},{96,112},{112,128},... | collective-permute-start | bytes 18440 | tf_op jit(solution)/shard_map/ppermute | solution.py:16
  24.6 30.0 %collective-permute-start.2 = (bf16[1,96,32]{1,2,0:T(8,128)(2,1)S(1)}, bf16[1,96,32]{1,2,0:T(8,128)(2,1)S(1)}, u32[]{:S(2)}, u32[]{:S(2)}) collective-permute-start(bf16[1,96,32]{1,2,0:T(8,128)(2,1)S(1)} %get-tuple-element.767), channel_id=1, source_target_pairs={{16,0},{32,16},{48,32},{64,48},{80,64},{96,80},{112,96},{128,112},... | collective-permute-start | bytes 18440 | tf_op jit(solution)/shard_map/ppermute | solution.py:16
  28.1 28.1 %collective-permute-start.1 = (bf16[1,96,32]{1,2,0:T(8,128)(2,1)S(1)}, bf16[1,96,32]{1,2,0:T(8,128)(2,1)S(1)}, u32[]{:S(2)}, u32[]{:S(2)}) collective-permute-start(bf16[1,96,32]{1,2,0:T(8,128)(2,1)S(1)} %get-tuple-element.768), channel_id=1, source_target_pairs={{0,64},{16,80},{32,96},{48,112},{64,128},{80,144},{96,160},{112,17... | collective-permute-start | bytes 18440 | tf_op jit(solution)/shard_map/ppermute | solution.py:16
  35.4 22.2 %collective-permute-start = (bf16[1,96,32]{1,2,0:T(8,128)(2,1)S(1)}, bf16[1,96,32]{1,2,0:T(8,128)(2,1)S(1)}, u32[]{:S(2)}, u32[]{:S(2)}) collective-permute-start(bf16[1,96,32]{1,2,0:T(8,128)(2,1)S(1)} %get-tuple-element.769), channel_id=1, source_target_pairs={{64,0},{80,16},{96,32},{112,48},{128,64},{144,80},{160,96},{176,11... | collective-permute-start | bytes 18440 | tf_op jit(solution)/shard_map/ppermute | solution.py:16
  54.7 16.5 %collective-permute-start.21 = (bf16[1,96,4]{1,2,0:T(4,128)(2,1)S(1)}, bf16[1,96,4]{1,2,0:T(4,128)(2,1)S(1)}, u32[]{:S(2)}, u32[]{:S(2)}) collective-permute-start(bf16[1,96,4]{1,2,0:T(4,128)(2,1)S(1)} %get-tuple-element.748), channel_id=1, source_target_pairs={{48,0},{64,16},{80,32},{96,48},{112,64},{128,80},{144,96},{160,112... | collective-permute-start | bytes 2312 | tf_op jit(solution)/shard_map/ppermute | solution.py:16
  56.3 44.4 %collective-permute-start.20 = (bf16[1,96,4]{1,2,0:T(4,128)(2,1)S(1)}, bf16[1,96,4]{1,2,0:T(4,128)(2,1)S(1)}, u32[]{:S(2)}, u32[]{:S(2)}) collective-permute-start(bf16[1,96,4]{1,2,0:T(4,128)(2,1)S(1)} %get-tuple-element.749), channel_id=1, source_target_pairs={{80,0},{96,16},{112,32},{128,48},{144,64},{160,80},{176,96},{192,1... | collective-permute-start | bytes 2312 | tf_op jit(solution)/shard_map/ppermute | solution.py:16
  57.6 43.1 %collective-permute-start.19 = (bf16[1,96,32]{1,2,0:T(8,128)(2,1)S(1)}, bf16[1,96,32]{1,2,0:T(8,128)(2,1)S(1)}, u32[]{:S(2)}, u32[]{:S(2)}) collective-permute-start(bf16[1,96,32]{1,2,0:T(8,128)(2,1)S(1)} %get-tuple-element.750), channel_id=1, source_target_pairs={{0,16},{16,32},{32,48},{48,64},{64,80},{80,96},{96,112},{112,128},... | collective-permute-start | bytes 18440 | tf_op jit(solution)/shard_map/ppermute | solution.py:16
  59.9 40.9 %collective-permute-start.18 = (bf16[1,96,32]{1,2,0:T(8,128)(2,1)S(1)}, bf16[1,96,32]{1,2,0:T(8,128)(2,1)S(1)}, u32[]{:S(2)}, u32[]{:S(2)}) collective-permute-start(bf16[1,96,32]{1,2,0:T(8,128)(2,1)S(1)} %get-tuple-element.751), channel_id=1, source_target_pairs={{16,0},{32,16},{48,32},{64,48},{80,64},{96,80},{112,96},{128,112},... | collective-permute-start | bytes 18440 | tf_op jit(solution)/shard_map/ppermute | solution.py:16
  63.0 37.8 %collective-permute-start.17 = (bf16[1,96,32]{1,2,0:T(8,128)(2,1)S(1)}, bf16[1,96,32]{1,2,0:T(8,128)(2,1)S(1)}, u32[]{:S(2)}, u32[]{:S(2)}) collective-permute-start(bf16[1,96,32]{1,2,0:T(8,128)(2,1)S(1)} %get-tuple-element.752), channel_id=1, source_target_pairs={{0,64},{16,80},{32,96},{48,112},{64,128},{80,144},{96,160},{112,17... | collective-permute-start | bytes 18440 | tf_op jit(solution)/shard_map/ppermute | solution.py:16
  71.2 29.6 %collective-permute-start.16 = (bf16[1,96,32]{1,2,0:T(8,128)(2,1)S(1)}, bf16[1,96,32]{1,2,0:T(8,128)(2,1)S(1)}, u32[]{:S(2)}, u32[]{:S(2)}) collective-permute-start(bf16[1,96,32]{1,2,0:T(8,128)(2,1)S(1)} %get-tuple-element.753), channel_id=1, source_target_pairs={{64,0},{80,16},{96,32},{112,48},{128,64},{144,80},{160,96},{176,11... | collective-permute-start | bytes 18440 | tf_op jit(solution)/shard_map/ppermute | solution.py:16
  130.8 45.5 %collective-permute-start.15 = (bf16[1,96,4]{1,2,0:T(4,128)(2,1)S(1)}, bf16[1,96,4]{1,2,0:T(4,128)(2,1)S(1)}, u32[]{:S(2)}, u32[]{:S(2)}) collective-permute-start(bf16[1,96,4]{1,2,0:T(4,128)(2,1)S(1)} %get-tuple-element.754), channel_id=1, source_target_pairs={{0,80},{16,96},{32,112},{48,128},{64,144},{80,160},{96,176},{112,1... | collective-permute-start | bytes 2312 | tf_op jit(solution)/shard_map/ppermute | solution.py:16
  137.4 41.6 %collective-permute-start.14 = (bf16[1,96,4]{1,2,0:T(4,128)(2,1)S(1)}, bf16[1,96,4]{1,2,0:T(4,128)(2,1)S(1)}, u32[]{:S(2)}, u32[]{:S(2)}) collective-permute-start(bf16[1,96,4]{1,2,0:T(4,128)(2,1)S(1)} %get-tuple-element.755), channel_id=1, source_target_pairs={{0,48},{16,64},{32,80},{48,96},{64,112},{80,128},{96,144},{112,160... | collective-permute-start | bytes 2312 | tf_op jit(solution)/shard_map/ppermute | solution.py:16
  140.6 45.8 %collective-permute-start.13 = (bf16[1,96,4]{1,2,0:T(4,128)(2,1)S(1)}, bf16[1,96,4]{1,2,0:T(4,128)(2,1)S(1)}, u32[]{:S(2)}, u32[]{:S(2)}) collective-permute-start(bf16[1,96,4]{1,2,0:T(4,128)(2,1)S(1)} %get-tuple-element.756), channel_id=1, source_target_pairs={{48,0},{64,16},{80,32},{96,48},{112,64},{128,80},{144,96},{160,112... | collective-permute-start | bytes 2312 | tf_op jit(solution)/shard_map/ppermute | solution.py:16
  141.9 47.3 %collective-permute-start.12 = (bf16[1,96,4]{1,2,0:T(4,128)(2,1)S(1)}, bf16[1,96,4]{1,2,0:T(4,128)(2,1)S(1)}, u32[]{:S(2)}, u32[]{:S(2)}) collective-permute-start(bf16[1,96,4]{1,2,0:T(4,128)(2,1)S(1)} %get-tuple-element.757), channel_id=1, source_target_pairs={{80,0},{96,16},{112,32},{128,48},{144,64},{160,80},{176,96},{192,1... | collective-permute-start | bytes 2312 | tf_op jit(solution)/shard_map/ppermute | solution.py:16
  143.2 52.6 %collective-permute-start.11 = (bf16[1,96,32]{1,2,0:T(8,128)(2,1)S(1)}, bf16[1,96,32]{1,2,0:T(8,128)(2,1)S(1)}, u32[]{:S(2)}, u32[]{:S(2)}) collective-permute-start(bf16[1,96,32]{1,2,0:T(8,128)(2,1)S(1)} %get-tuple-element.758), channel_id=1, source_target_pairs={{0,16},{16,32},{32,48},{48,64},{64,80},{80,96},{96,112},{112,128},... | collective-permute-start | bytes 18440 | tf_op jit(solution)/shard_map/ppermute | solution.py:16
  176.3 23.5 %collective-permute-start.10 = (bf16[1,96,32]{1,2,0:T(8,128)(2,1)S(1)}, bf16[1,96,32]{1,2,0:T(8,128)(2,1)S(1)}, u32[]{:S(2)}, u32[]{:S(2)}) collective-permute-start(bf16[1,96,32]{1,2,0:T(8,128)(2,1)S(1)} %get-tuple-element.759), channel_id=1, source_target_pairs={{16,0},{32,16},{48,32},{64,48},{80,64},{96,80},{112,96},{128,112},... | collective-permute-start | bytes 18440 | tf_op jit(solution)/shard_map/ppermute | solution.py:16
  179.0 22.1 %collective-permute-start.9 = (bf16[1,96,32]{1,2,0:T(8,128)(2,1)S(1)}, bf16[1,96,32]{1,2,0:T(8,128)(2,1)S(1)}, u32[]{:S(2)}, u32[]{:S(2)}) collective-permute-start(bf16[1,96,32]{1,2,0:T(8,128)(2,1)S(1)} %get-tuple-element.760), channel_id=1, source_target_pairs={{0,64},{16,80},{32,96},{48,112},{64,128},{80,144},{96,160},{112,17... | collective-permute-start | bytes 18440 | tf_op jit(solution)/shard_map/ppermute | solution.py:16
  189.2 75.4 %collective-permute-start.31 = (bf16[1,96,4]{1,2,0:T(4,128)(2,1)S(1)}, bf16[1,96,4]{1,2,0:T(4,128)(2,1)S(1)}, u32[]{:S(2)}, u32[]{:S(2)}) collective-permute-start(bf16[1,96,4]{1,2,0:T(4,128)(2,1)S(1)} %get-tuple-element.738), channel_id=1, source_target_pairs={{0,80},{16,96},{32,112},{48,128},{64,144},{80,160},{96,176},{112,1... | collective-permute-start | bytes 2312 | tf_op jit(solution)/shard_map/ppermute | solution.py:16
  195.8 72.4 %collective-permute-start.30 = (bf16[1,96,4]{1,2,0:T(4,128)(2,1)S(1)}, bf16[1,96,4]{1,2,0:T(4,128)(2,1)S(1)}, u32[]{:S(2)}, u32[]{:S(2)}) collective-permute-start(bf16[1,96,4]{1,2,0:T(4,128)(2,1)S(1)} %get-tuple-element.739), channel_id=1, source_target_pairs={{0,48},{16,64},{32,80},{48,96},{64,112},{80,128},{96,144},{112,160... | collective-permute-start | bytes 2312 | tf_op jit(solution)/shard_map/ppermute | solution.py:16
  199.8 75.6 %collective-permute-start.29 = (bf16[1,96,4]{1,2,0:T(4,128)(2,1)S(1)}, bf16[1,96,4]{1,2,0:T(4,128)(2,1)S(1)}, u32[]{:S(2)}, u32[]{:S(2)}) collective-permute-start(bf16[1,96,4]{1,2,0:T(4,128)(2,1)S(1)} %get-tuple-element.740), channel_id=1, source_target_pairs={{48,0},{64,16},{80,32},{96,48},{112,64},{128,80},{144,96},{160,112... | collective-permute-start | bytes 2312 | tf_op jit(solution)/shard_map/ppermute | solution.py:16
  201.1 77.2 %collective-permute-start.28 = (bf16[1,96,4]{1,2,0:T(4,128)(2,1)S(1)}, bf16[1,96,4]{1,2,0:T(4,128)(2,1)S(1)}, u32[]{:S(2)}, u32[]{:S(2)}) collective-permute-start(bf16[1,96,4]{1,2,0:T(4,128)(2,1)S(1)} %get-tuple-element.741), channel_id=1, source_target_pairs={{80,0},{96,16},{112,32},{128,48},{144,64},{160,80},{176,96},{192,1... | collective-permute-start | bytes 2312 | tf_op jit(solution)/shard_map/ppermute | solution.py:16
  202.5 75.9 %collective-permute-start.27 = (bf16[1,96,32]{1,2,0:T(8,128)(2,1)S(1)}, bf16[1,96,32]{1,2,0:T(8,128)(2,1)S(1)}, u32[]{:S(2)}, u32[]{:S(2)}) collective-permute-start(bf16[1,96,32]{1,2,0:T(8,128)(2,1)S(1)} %get-tuple-element.742), channel_id=1, source_target_pairs={{0,16},{16,32},{32,48},{48,64},{64,80},{80,96},{96,112},{112,128},... | collective-permute-start | bytes 18440 | tf_op jit(solution)/shard_map/ppermute | solution.py:16
  (16 other events, 242.7 us)
Sparse Core Ops, SparseCore 0:
  278.5 489.0 all-reduce.6
where the time goes:
time: 781 us; the launch traced here: 778 us
  waiting for transfers between devices  462 us (59%)
  local copies, waits for them, and re-layouts  180 us (23%)
  starting transfers between devices  106 us (14%)
  between operations  14.9 us (2%)
  matrix products  11.6 us (1%)
    psum x1, waiting for transfers between devices, body(): lax.psum((first_grad, second_grad), ('blk', 'smp'))  453 us
    gather x41, local copies, waits for them, and re-layouts, gather_columns(): portion[:, indices]  166 us
    ppermute x32, starting transfers between devices, from_behind(): return lax.ppermute(shard, axis, pairs)  106 us
  transfers between devices with their start and end apart: 33, of which 3 were waited for; matrix products, arithmetic and copies ran while one was open for 20% of the time, Pallas kernels for 0%

commit v1 on v0

v1 whole, which is shorter than its diff:
```python
import functools

import jax
import jax.numpy as jnp
from jax import lax
from jax.experimental import pallas as pl
from jax.experimental.pallas import tpu as pltpu
from jax.sharding import PartitionSpec as P

MESH = pl.DeviceIdType.MESH
TALL = 4
STEPS = ((-1, 0), (1, 0), (0, -1), (0, 1), (-1, -1), (-1, 1), (1, -1), (1, 1))
DELTAS = tuple(a * TALL + b for a, b in STEPS)
OFFSETS = 27
GROUP = 4
GROUPS = 7
CORNER = 16
UNROLL = 3


def nn(a, b):
    return lax.dot_general(a, b, (((1,), (0,)), ((), ())), preferred_element_type=jnp.float32)


def nt(a, b):
    return lax.dot_general(a, b, (((1,), (1,)), ((), ())), preferred_element_type=jnp.float32)


def eye(n, dtype):
    rows = lax.broadcasted_iota(jnp.int32, (n, n), 0)
    cols = lax.broadcasted_iota(jnp.int32, (n, n), 1)
    return (rows == cols).astype(jnp.float32).astype(dtype)


def one_hot(rows, codes):
    return jnp.where(rows == codes, 1.0, 0.0).astype(jnp.bfloat16)


def main_kernel(
    nb, nz,
    feat, act, nbr, lists, w1, w2, cot,
    out_field, input_grad, gathered,
    field, pick, sent_a, halo_a, sent_c, halo_c,
    local_hot, halo_hot, turned, picked, sides,
    to_core, own, from_core, summed, arrived, z_part, z_in, z_out,
    sem_a, sem_c, sem_core, sem_plane, sem_z, sem_zg, sem_gather, sem_forward,
):
    bf16, f32 = jnp.bfloat16, jnp.float32
    channels, voxels = feat.shape[1], feat.shape[2]
    both = 2 * channels
    per_list = lists.shape[3]
    halo_rows = halo_a.shape[0]
    nj = nb // 2
    half_rows = own.shape[0]
    piece = half_rows // nj
    sliver = piece // nz
    group_rows = GROUP * channels * channels // 128
    blk = lax.axis_index("blk")
    smp = lax.axis_index("smp")
    core = lax.rem(blk, 2)
    chip = lax.div(blk, 2)
    other = 1 - core
    partner = (chip * 2 + other, smp)

    def plane(i):
        return lax.rem(chip + i, nj)

    def along(i):
        return lax.rem(smp + i, nz)

    def remote(src, dst, sems, source, target, device):
        return pltpu.make_async_remote_copy(
            src_ref=src, dst_ref=dst, send_sem=sems.at[0, target], recv_sem=sems.at[1, source],
            device_id=device, device_id_type=MESH,
        )

    halo_a[...] = jnp.zeros_like(halo_a)
    halo_c[...] = jnp.zeros_like(halo_c)
    barrier = pltpu.get_barrier_semaphore()

    def greet_blk(i, _):
        pl.semaphore_signal(
            barrier, inc=1, device_id=(lax.rem(blk + i, nb), smp), device_id_type=MESH
        )
        return 0

    def greet_smp(i, _):
        pl.semaphore_signal(barrier, inc=1, device_id=(blk, along(i)), device_id_type=MESH)
        return 0

    lax.fori_loop(1, nb, greet_blk, 0)
    lax.fori_loop(1, nz, greet_smp, 0)

    live = act[...] > 0
    live_f = live.astype(f32)
    field[0:channels, :] = jnp.where(live, feat[0].astype(f32), 0.0).astype(bf16)
    field[channels:both, :] = jnp.where(live, cot[0].astype(f32), 0.0).astype(bf16)

    spread = jnp.concatenate(
        [jnp.broadcast_to(lists[0, 0, d : d + 1, :], (per_list, per_list)) for d in range(8)], axis=0
    )
    at_row = lax.broadcasted_iota(jnp.int32, spread.shape, 0)
    at_col = lax.broadcasted_iota(jnp.int32, spread.shape, 1)
    column = jnp.sum(jnp.where(lax.rem(at_row, per_list) == at_col, spread, 0), axis=1, keepdims=True)
    pick[...] = one_hot(lax.broadcasted_iota(jnp.int32, (8 * per_list, voxels), 1), column)

    def face_copies(sent, halo, sems):
        copies = []
        for d, delta in enumerate(DELTAS):
            if d < 4:
                rows = pl.ds(d * per_list, per_list)
                into = rows
            else:
                rows = pl.ds(d * per_list, CORNER)
                into = pl.ds(4 * per_list + (d - 4) * CORNER, CORNER)
            target, source = blk + delta, blk - delta
            copy = pltpu.make_async_remote_copy(
                src_ref=sent.at[rows, :], dst_ref=halo.at[into, :],
                send_sem=sems.at[0, d], recv_sem=sems.at[1, d],
                device_id=(jnp.clip(target, 0, nb - 1), smp), device_id_type=MESH,
            )
            has_target = (target >= 0) & (target < nb)
            has_source = (source >= 0) & (source < nb)
            copies.append((copy, has_target, has_source))
        return copies

    def start_faces(copies):
        for copy, has_target, _ in copies:
            pl.when(has_target)(copy.start)

    def arrive_faces(copies):
        for copy, _, has_source in copies:
            pl.when(has_source)(copy.wait_recv)

    def finish_faces(copies):
        for copy, has_target, _ in copies:
            pl.when(has_target)(copy.wait_send)

    faces_a = face_copies(sent_a, halo_a, sem_a)
    faces_c = face_copies(sent_c, halo_c, sem_c)
    sent_a[:, 0:both] = nt(pick[...], field[...]).astype(bf16)
    sent_a[:, both:] = jnp.zeros((8 * per_list, sent_a.shape[1] - both), bf16)
    pl.semaphore_wait(barrier, (nb - 1) + (nz - 1))
    start_faces(faces_a)

    unit = eye(channels, bf16)
    local_rows = lax.broadcasted_iota(jnp.int32, (voxels, voxels), 0)
    place = lax.broadcasted_iota(jnp.int32, (halo_rows, voxels), 0)
    past = place - 4 * per_list
    corner_code = jnp.where(
        lax.rem(past, CORNER) < 4, voxels + 4 * per_list + lax.div(past, CORNER) * 4 + lax.rem(past, CORNER), -1
    )
    halo_codes = jnp.where(past < 0, voxels + place, corner_code)

    def at(o):
        return pl.ds(pl.multiple_of(o * channels, 32), channels)

    def prepare(step, _):
        for u in range(UNROLL):
            o = step * UNROLL + u
            codes = nbr[0, pl.ds(o, 1), :]
            hot = one_hot(local_rows, codes)
            local_hot[o] = hot
            halo_hot[o] = one_hot(halo_codes, codes)
            got = nn(field[...], hot).astype(bf16)
            picked[0, at(o), :] = got[:channels]
            picked[1, at(OFFSETS - 1 - o), :] = got[channels:]
            turned[0, o] = nt(unit, w1[o]).astype(bf16)
            turned[1, o] = nt(unit, w2[o]).astype(bf16)
        return 0

    lax.fori_loop(0, OFFSETS // UNROLL, prepare, 0)
    tail = picked.shape[1] - OFFSETS * channels
    picked[:, OFFSETS * channels :, :] = jnp.zeros((2, tail, voxels), bf16)
    rest = half_rows - GROUPS * group_rows
    own[GROUPS * group_rows :, :] = jnp.zeros((rest, 128), f32)
    summed[GROUPS * group_rows :, :] = jnp.zeros((rest, 128), bf16)

    arrive_faces(faces_a)
    turned_halo = nt(eye(halo_a.shape[1], bf16)[:both], halo_a[...]).astype(bf16)
    zeros = jnp.zeros((channels, voxels), f32)

    def first_pass(step, sums):
        forth, back = sums
        for u in range(UNROLL):
            o = step * UNROLL + u
            mirror = OFFSETS - 1 - o
            got = nn(turned_halo, halo_hot[o]).astype(bf16)
            mine = picked[0, at(o), :] + got[:channels]
            theirs = picked[1, at(mirror), :] + got[channels:]
            picked[0, at(o), :] = mine
            picked[1, at(mirror), :] = theirs
            forth = forth + nn(w1[o], mine)
            back = back + nn(turned[1, mirror], theirs)
        return forth, back

    forth, back = lax.fori_loop(0, OFFSETS // UNROLL, first_pass, (zeros, zeros))
    pre = live_f * forth
    gate = 1.0 / (1.0 + jnp.exp(-pre))
    hidden = (live_f * (pre * gate)).astype(bf16)
    grad_pre = ((live_f * back) * gate * (1.0 + pre * (1.0 - gate))).astype(bf16)
    sides[0] = grad_pre
    sides[1] = hidden
    field[0:channels, :] = hidden
    field[channels:both, :] = grad_pre
    sent_c[:, 0:both] = nt(pick[...], field[...]).astype(bf16)
    sent_c[:, both:] = jnp.zeros((8 * per_list, sent_c.shape[1] - both), bf16)
    start_faces(faces_c)

    def core_copy(g):
        rows = pl.ds(pl.multiple_of(g * group_rows, 32), group_rows)
        return remote(to_core.at[rows, :], from_core.at[rows, :], sem_core, g, g, partner)

    def correlate(which, g):
        rows = pl.ds(pl.multiple_of(g * (GROUP * channels), 128), GROUP * channels)
        return nt(sides[which], picked[which, rows, :])

    def give(g, _):
        product = correlate(other, g)
        for t in range(group_rows // channels):
            rows = pl.ds(pl.multiple_of(g * group_rows + t * channels, 32), channels)
            to_core[rows, :] = product[:, t * 128 : (t + 1) * 128].astype(bf16)
        core_copy(g).start()
        return 0

    def keep(g, _):
        product = correlate(core, g)
        for t in range(group_rows // channels):
            rows = pl.ds(pl.multiple_of(g * group_rows + t * channels, 32), channels)
            own[rows, :] = product[:, t * 128 : (t + 1) * 128]
        return 0

    def join(g, _):
        core_copy(g).wait_recv()
        rows = pl.ds(pl.multiple_of(g * group_rows, 32), group_rows)
        total = own[rows, :] + from_core[rows, :].astype(f32)
        own[rows, :] = total
        summed[rows, :] = total.astype(bf16)
        return 0

    lax.fori_loop(0, GROUPS, give, 0)
    lax.fori_loop(0, GROUPS, keep, 0)
    lax.fori_loop(0, GROUPS, join, 0)

    def piece_rows(p):
        return pl.ds(pl.multiple_of(p * piece, piece), piece)

    def plane_copy(source, target):
        return remote(
            summed.at[piece_rows(target), :], arrived.at[source], sem_plane, source, target,
            (target * 2 + core, smp),
        )

    def loop(start, stop, act_on):
        def run(i, _):
            act_on(i)
            return 0

        lax.fori_loop(start, stop, run, 0)

    loop(1, nj, lambda i: plane_copy(chip, plane(i)).start())

    arrive_faces(faces_c)
    turned_halo_c = nt(eye(halo_c.shape[1], bf16)[:both], halo_c[...]).astype(bf16)

    def second_pass(step, sums):
        forth, back = sums
        for u in range(UNROLL):
            o = step * UNROLL + u
            got = (nn(field[...], local_hot[o]) + nn(turned_halo_c, halo_hot[o])).astype(bf16)
            forth = forth + nn(w2[o], got[:channels])
            back = back + nn(turned[0, OFFSETS - 1 - o], got[channels:])
        return forth, back

    forth, back = lax.fori_loop(0, OFFSETS // UNROLL, second_pass, (zeros, zeros))
    out_field[...] = (live_f * forth).astype(bf16)
    input_grad[...] = (live_f * back).astype(bf16)

    z_part[...] = own[piece_rows(chip), :]

    def add_piece(i):
        source = plane(i)
        plane_copy(source, source).wait_recv()
        z_part[...] += arrived[source].astype(f32)

    loop(1, nj, add_piece)

    def sliver_rows(s):
        return pl.ds(pl.multiple_of(s * sliver, 8), sliver)

    def z_copy(source, target):
        return remote(
            z_part.at[sliver_rows(target), :], z_in.at[source], sem_z, source, target, (blk, target)
        )

    def zg_copy(source, target):
        return remote(
            z_out.at[sliver_rows(source), :], z_out.at[sliver_rows(source), :], sem_zg, source, target,
            (blk, target),
        )

    loop(1, nz, lambda i: z_copy(smp, along(i)).start())
    z_in[smp] = z_part[sliver_rows(smp), :]
    loop(1, nz, lambda i: z_copy(along(i), along(i)).wait_recv())
    total = z_in[0]
    for s in range(1, nz):
        total = total + z_in[s]
    z_out[sliver_rows(smp), :] = total
    loop(1, nz, lambda i: zg_copy(smp, along(i)).start())
    loop(1, nz, lambda i: zg_copy(along(i), along(i)).wait_recv())

    def gather_copy(source, target):
        here = gathered.at[core, piece_rows(source), :]
        return remote(here, here, sem_gather, source, target, (target * 2 + core, smp))

    def forward_copy(which, p):
        here = gathered.at[which, piece_rows(p), :]
        return remote(here, here, sem_forward, p, p, partner)

    gathered[core, piece_rows(chip), :] = z_out[...].astype(bf16)
    loop(1, nj, lambda i: gather_copy(chip, plane(i)).start())
    forward_copy(core, chip).start()

    def hand_on(i):
        source = plane(i)
        gather_copy(source, source).wait_recv()
        forward_copy(core, source).start()

    loop(1, nj, hand_on)
    loop(0, nj, lambda p: forward_copy(other, p).wait_recv())

    finish_faces(faces_a)
    finish_faces(faces_c)
    loop(0, GROUPS, lambda g: core_copy(g).wait_send())
    loop(1, nj, lambda i: plane_copy(chip, plane(i)).wait_send())
    loop(1, nz, lambda i: z_copy(smp, along(i)).wait_send())
    loop(1, nz, lambda i: zg_copy(smp, along(i)).wait_send())
    loop(1, nj, lambda i: gather_copy(chip, plane(i)).wait_send())
    loop(0, nj, lambda p: forward_copy(core, p).wait_send())


def unpack_kernel(scale, sums, field_in, grad_in, first, second, field_out, grad_out):
    channels = first.shape[1]
    field_out[0] = field_in[...]
    grad_out[0] = grad_in[...]
    unit = eye(channels, jnp.bfloat16)
    tiles = GROUP * channels // 128
    for which, out in enumerate((first, second)):
        wide = jnp.concatenate(
            [sums[which, t * channels : (t + 1) * channels, :] for t in range(tiles)], axis=1
        )
        for k in range(GROUP):
            block = wide[:, k * channels : (k + 1) * channels]
            block = nt(unit, block) if which else block.astype(jnp.float32)
            out[k] = block * scale


def body(nb, nz, features, active, neighbour_rows, send_rows, first_weight, second_weight, cotangent):
    channels, voxels = features.shape[1], features.shape[2]
    both = 2 * channels
    per_list = send_rows.shape[3]
    halo_rows = 4 * per_list + 4 * CORNER
    nj = nb // 2
    half_rows = 2048
    piece = half_rows // nj
    bf16, f32 = jnp.bfloat16, jnp.float32
    vmem = pl.BlockSpec(memory_space=pltpu.VMEM)
    dma = pltpu.SemaphoreType.DMA
    wide = 256
    out_field, input_grad, gathered = pl.pallas_call(
        functools.partial(main_kernel, nb, nz),
        out_shape=[
            jax.ShapeDtypeStruct((channels, voxels), bf16),
            jax.ShapeDtypeStruct((channels, voxels), bf16),
            jax.ShapeDtypeStruct((2, half_rows, 128), bf16),
        ],
        in_specs=[vmem] * 7,
        out_specs=[vmem] * 3,
        scratch_shapes=[
            pltpu.VMEM((both, voxels), bf16),
            pltpu.VMEM((8 * per_list, voxels), bf16),
            pltpu.VMEM((8 * per_list, wide), bf16),
            pltpu.VMEM((halo_rows, wide), bf16),
            pltpu.VMEM((8 * per_list, wide), bf16),
            pltpu.VMEM((halo_rows, wide), bf16),
            pltpu.VMEM((OFFSETS, voxels, voxels), bf16),
            pltpu.VMEM((OFFSETS, halo_rows, voxels), bf16),
            pltpu.VMEM((2, OFFSETS, channels, channels), bf16),
            pltpu.VMEM((2, GROUP * GROUPS * channels, voxels), bf16),
            pltpu.VMEM((2, channels, voxels), bf16),
            pltpu.VMEM((half_rows, 128), bf16),
            pltpu.VMEM((half_rows, 128), f32),
            pltpu.VMEM((half_rows, 128), bf16),
            pltpu.VMEM((half_rows, 128), bf16),
            pltpu.VMEM((nj, piece, 128), bf16),
            pltpu.VMEM((piece, 128), f32),
            pltpu.VMEM((nz, piece // nz, 128), f32),
            pltpu.VMEM((piece, 128), f32),
            dma((2, 8)),
            dma((2, 8)),
            dma((2, GROUPS)),
            dma((2, nj)),
            dma((2, nz)),
            dma((2, nz)),
            dma((2, nj)),
            dma((2, nj)),
        ],
        compiler_params=pltpu.CompilerParams(
            collective_id=0, has_side_effects=True, vmem_limit_bytes=40 * 2**20
        ),
        name="halo_conv_and_sum",
    )(features, active, neighbour_rows, send_rows, first_weight, second_weight, cotangent)

    slots = lax.axis_size("smp") * features.shape[0] * nb * voxels
    group_rows = GROUP * channels * channels // 128
    whole = pl.BlockSpec((channels, voxels), lambda g: (0, 0))
    whole_out = pl.BlockSpec((1, channels, voxels), lambda g: (0, 0, 0))
    grads = pl.BlockSpec((GROUP, channels, channels), lambda g: (g, 0, 0))
    first_grad, second_grad, out_field, input_grad = pl.pallas_call(
        functools.partial(unpack_kernel, 1.0 / slots**0.5),
        grid=(GROUPS,),
        out_shape=[
            jax.ShapeDtypeStruct((OFFSETS, channels, channels), f32),
            jax.ShapeDtypeStruct((OFFSETS, channels, channels), f32),
            jax.ShapeDtypeStruct((1, channels, voxels), bf16),
            jax.ShapeDtypeStruct((1, channels, voxels), bf16),
        ],
        in_specs=[pl.BlockSpec((2, group_rows, 128), lambda g: (0, g, 0)), whole, whole],
        out_specs=[grads, grads, whole_out, whole_out],
        name="unpack",
    )(gathered, out_field, input_grad)
    return out_field, input_grad, first_grad, second_grad


def solution(mesh):
    return jax.shard_map(
        functools.partial(body, mesh.shape["blk"], mesh.shape["smp"]),
        mesh=mesh,
        in_specs=(
            P("smp", None, "blk"),
            P("smp", "blk"),
            P("smp", None, "blk"),
            P("smp", "blk", None, None),
            P(),
            P(),
            P("smp", None, "blk"),
        ),
        out_specs=(P("smp", None, "blk"), P("smp", None, "blk"), P(), P()),
        check_vma=False,
    )
```

time: 781 us -> 82.5 us (0.11)
  waiting for transfers between devices: 462 us -> 0 us
  local copies, waits for them, and re-layouts: 180 us -> 8.1 us
  starting transfers between devices: 106 us -> 0 us
  Pallas kernels: 0 us -> 73.2 us
  between operations: 14.9 us -> 0.66 us
  matrix products: 11.6 us -> 0 us
    psum x1 -> x0, waiting for transfers between devices: 453 us -> none  [body(): lax.psum((first_grad, second_grad), ('blk', 'smp'))]
    gather x41 -> x0, local copies, waits for them, and re-layouts: 166 us -> none  [gather_columns(): portion[:, indices]]
    ppermute x32 -> x0, starting transfers between devices: 106 us -> none  [from_behind(): return lax.ppermute(shard, axis, pairs)]
    pallas_call x0 -> x2, Pallas kernels: none -> 73.2 us  [the longest x1 67.3 us: body(): pl.pallas_call(functools.partial(main_kernel, nb, nz), out_shape=[jax.Sha...]
    dot_general x18 -> x0, matrix products: 11.6 us -> none  [the longest x12 9.62 us: convolve_accumulate(): jnp.einsum('oik,skov->siv', matrices, picked, preferred_element_type=jnp....]
    ppermute x32 -> x0, waiting for transfers between devices: 8.54 us -> none  [from_behind(): return lax.ppermute(shard, axis, pairs)]
  transfers between devices with their start and end apart: 33 -> 0, of which waited for: 3 -> 0; matrix products, arithmetic and copies ran while one was open for 20% -> 0% of each run, Pallas kernels for 0% -> 0%
where the time goes in v1:
time: 82.5 us; the launch traced here: 82 us
  Pallas kernels  73.2 us (89%)
  local copies, waits for them, and re-layouts  8.1 us (10%)
    pallas_call x1, Pallas kernels, body(): pl.pallas_call(functools.partial(main_kernel, nb, nz), out_shape=[jax.Sha...  67.3 us
    unnamed x19, local copies, waits for them, and re-layouts  8.1 us
    pallas_call x1, Pallas kernels, body(): pl.pallas_call(functools.partial(unpack_kernel, 1.0 / slots ** 0.5), grid...  5.92 us

profile of v1, /device:TPU:1, one launch (start us, length us, event | category | flops | bytes accessed | tf_op | source)
XLA Modules:
  0.0 82.0 jit_solution(5671821980506477290)
XLA Ops:
  0.6 0.7 copy.11.nbr
  1.4 0.0 copy-start.1
  1.4 1.1 %copy-done.1 = bf16[27,96,96]{2,1,0:T(8,128)(2,1)S(1)} copy-done((bf16[27,96,96]{2,1,0:T(8,128)(2,1)S(1)}, bf16[27,96,96]{2,1,0:T(8,128)(2,1)}, u32[]{:S(2)}) %copy-start.1) | copy-done | bytes 497688
  2.5 0.0 copy-start.2
  2.5 1.1 %copy-done.2 = bf16[27,96,96]{2,1,0:T(8,128)(2,1)S(1)} copy-done((bf16[27,96,96]{2,1,0:T(8,128)(2,1)S(1)}, bf16[27,96,96]{2,1,0:T(8,128)(2,1)}, u32[]{:S(2)}) %copy-start.2) | copy-done | bytes 497688
  3.6 0.0 copy-start.3
  3.6 0.8 copy-done.3
  4.4 0.0 copy-start.4
  4.4 0.8 copy-done.4
  5.2 0.0 copy-start.7
  5.2 0.7 copy-done.7
  5.8 0.0 copy-start.8
  5.8 0.7 copy-done.8
  6.5 67.3 %halo_conv_and_sum.1 = (bf16[96,256]{1,0:T(8,128)(2,1)S(1)}, bf16[96,256]{1,0:T(8,128)(2,1)S(1)}, bf16[2,2048,128]{2,1,0:T(8,128)(2,1)S(1)}) custom-call(bf16[1,96,256]{2,1,0:T(8,128)(2,1)S(1)} %copy-done.3, s32[1,256]{1,0:T(1,128)S(1)} %copy-done.8, s32[1,27,256]{2,1,0:T(8,128)S(1)} %copy.11.nbr, s32[1,1,8,32]{3,2,1,0:T(8,128)S(1)} %copy-done.7, ...), custom_call_target="tpu_custom_call" | custom-call | tf_op jit(solution)/shard_map/halo_conv_and_sum/pallas_call | solution.py:370
  73.8 0.0 copy-start
  73.8 1.0 %copy-done = bf16[2,2048,128]{2,1,0:T(8,128)(2,1)} copy-done((bf16[2,2048,128]{2,1,0:T(8,128)(2,1)}, bf16[2,2048,128]{2,1,0:T(8,128)(2,1)S(1)}, u32[]{:S(2)}) %copy-start) | copy-done | bytes 1048600
  74.8 0.0 copy-start.5
  74.8 0.6 copy-done.5
  75.4 0.0 copy-start.6
  75.4 0.6 copy-done.6
  76.0 5.9 %unpack.1 = (f32[27,96,96]{2,1,0:T(8,128)}, f32[27,96,96]{2,1,0:T(8,128)}, bf16[1,96,256]{2,1,0:T(8,128)(2,1)}, bf16[1,96,256]{2,1,0:T(8,128)(2,1)}) custom-call(bf16[2,2048,128]{2,1,0:T(8,128)(2,1)} %copy-done, bf16[96,256]{1,0:T(8,128)(2,1)} %copy-done.5, bf16[96,256]{1,0:T(8,128)(2,1)} %copy-done.6), custom_call_target="tpu_custom_call" | custom-call | tf_op jit(solution)/shard_map/unpack/pallas_call | solution.py:419
Async XLA Ops:
  1.4 1.1 %copy-start.1 = (bf16[27,96,96]{2,1,0:T(8,128)(2,1)S(1)}, bf16[27,96,96]{2,1,0:T(8,128)(2,1)}, u32[]{:S(2)}) copy-start(bf16[27,96,96]{2,1,0:T(8,128)(2,1)} %w1.1) | copy-start | bytes 1492996
  2.5 1.1 %copy-start.2 = (bf16[27,96,96]{2,1,0:T(8,128)(2,1)S(1)}, bf16[27,96,96]{2,1,0:T(8,128)(2,1)}, u32[]{:S(2)}) copy-start(bf16[27,96,96]{2,1,0:T(8,128)(2,1)} %w2.1) | copy-start | bytes 1492996
  3.6 0.8 copy-start.3
  4.4 0.8 copy-start.4
  5.2 0.7 copy-start.7
  5.8 0.7 copy-start.8
  73.8 1.0 %copy-start = (bf16[2,2048,128]{2,1,0:T(8,128)(2,1)}, bf16[2,2048,128]{2,1,0:T(8,128)(2,1)S(1)}, u32[]{:S(2)}) copy-start(bf16[2,2048,128]{2,1,0:T(8,128)(2,1)S(1)} %get-tuple-element.11.sums) | copy-start | bytes 3145732
  74.8 0.6 copy-start.5
  75.4 0.6 copy-start.6

commit v2 on v1

--- a/solution.py
+++ b/solution.py
@@ -36,14 +36,21 @@
     return jnp.where(rows == codes, 1.0, 0.0).astype(jnp.bfloat16)
 
 
+def far_quarter(smp, nz):
+    per_quarter = nz // 4
+    late = lax.rem(smp, per_quarter) >= per_quarter // 2
+    return lax.rem(lax.div(smp, per_quarter) + jnp.where(late, 2, 1), 4)
+
+
 def main_kernel(
     nb, nz,
-    feat, act, nbr, lists, w1, w2, cot,
+    feat_in, act_in, nbr_in, lists_in, w1_in, w2_in, cot_in,
     out_field, input_grad, gathered,
+    feat, act, nbr, lists, w1, w2, cot, results, spreading,
     field, pick, sent_a, halo_a, sent_c, halo_c,
     local_hot, halo_hot, turned, picked, sides,
     to_core, own, from_core, summed, arrived, z_part, z_in, z_out,
-    sem_a, sem_c, sem_core, sem_plane, sem_z, sem_zg, sem_gather, sem_forward,
+    sem_in, sem_out, sem_a, sem_c, sem_core, sem_plane, sem_z, sem_zg, sem_gather, sem_keep, sem_forward,
 ):
     bf16, f32 = jnp.bfloat16, jnp.float32
     channels, voxels = feat.shape[1], feat.shape[2]
@@ -54,7 +61,10 @@
     half_rows = own.shape[0]
     piece = half_rows // nj
     sliver = piece // nz
+    quarter = piece // 4
+    some = piece // 2
     group_rows = GROUP * channels * channels // 128
+    tiles = GROUP * channels // 128
     blk = lax.axis_index("blk")
     smp = lax.axis_index("smp")
     core = lax.rem(blk, 2)
@@ -62,6 +72,16 @@
     other = 1 - core
     partner = (chip * 2 + other, smp)
 
+    def loop(start, stop, act_on):
+        def run(i, _):
+            act_on(i)
+            return 0
+
+        lax.fori_loop(start, stop, run, 0)
+
+    far = far_quarter(smp, nz)
+    near = lax.rem(far + 2, 4)
+
     def plane(i):
         return lax.rem(chip + i, nj)
 
@@ -74,6 +94,14 @@
             device_id=device, device_id_type=MESH,
         )
 
+    loads = [
+        pltpu.make_async_copy(src, dst, sem_in.at[i])
+        for i, (src, dst) in enumerate(
+            ((feat_in, feat), (cot_in, cot), (act_in, act), (lists_in, lists), (nbr_in, nbr), (w1_in, w1), (w2_in, w2))
+        )
+    ]
+    for load in loads:
+        load.start()
     halo_a[...] = jnp.zeros_like(halo_a)
     halo_c[...] = jnp.zeros_like(halo_c)
     barrier = pltpu.get_barrier_semaphore()
@@ -91,6 +119,8 @@
     lax.fori_loop(1, nb, greet_blk, 0)
     lax.fori_loop(1, nz, greet_smp, 0)
 
+    for load in loads[:4]:
+        load.wait()
     live = act[...] > 0
     live_f = live.astype(f32)
     field[0:channels, :] = jnp.where(live, feat[0].astype(f32), 0.0).astype(bf16)
@@ -143,6 +173,8 @@
     pl.semaphore_wait(barrier, (nb - 1) + (nz - 1))
     start_faces(faces_a)
 
+    for load in loads[4:]:
+        load.wait()
     unit = eye(channels, bf16)
     local_rows = lax.broadcasted_iota(jnp.int32, (voxels, voxels), 0)
     place = lax.broadcasted_iota(jnp.int32, (halo_rows, voxels), 0)
@@ -158,7 +190,7 @@
     def prepare(step, _):
         for u in range(UNROLL):
             o = step * UNROLL + u
-            codes = nbr[0, pl.ds(o, 1), :]
+            codes = nbr[o]
             hot = one_hot(local_rows, codes)
             local_hot[o] = hot
             halo_hot[o] = one_hot(halo_codes, codes)
@@ -174,7 +206,7 @@
     picked[:, OFFSETS * channels :, :] = jnp.zeros((2, tail, voxels), bf16)
     rest = half_rows - GROUPS * group_rows
     own[GROUPS * group_rows :, :] = jnp.zeros((rest, 128), f32)
-    summed[GROUPS * group_rows :, :] = jnp.zeros((rest, 128), bf16)
+    from_core[GROUPS * group_rows :, :] = jnp.zeros((rest, 128), bf16)
 
     arrive_faces(faces_a)
     turned_halo = nt(eye(halo_a.shape[1], bf16)[:both], halo_a[...]).astype(bf16)
@@ -213,52 +245,66 @@
 
     def correlate(which, g):
         rows = pl.ds(pl.multiple_of(g * (GROUP * channels), 128), GROUP * channels)
-        return nt(sides[which], picked[which, rows, :])
-
-    def give(g, _):
-        product = correlate(other, g)
-        for t in range(group_rows // channels):
-            rows = pl.ds(pl.multiple_of(g * group_rows + t * channels, 32), channels)
-            to_core[rows, :] = product[:, t * 128 : (t + 1) * 128].astype(bf16)
+        if which == 0:
+            return nt(sides[0], picked[0, rows, :])
+        tall = nt(picked[1, rows, :], sides[1])
+        return jnp.concatenate([tall[k * channels : (k + 1) * channels] for k in range(GROUP)], axis=1)
+
+    def tile_rows(g, t):
+        return pl.ds(pl.multiple_of(g * group_rows + t * channels, 32), channels)
+
+    def give(which, g):
+        product = correlate(which, g)
+        for t in range(tiles):
+            to_core[tile_rows(g, t), :] = product[:, t * 128 : (t + 1) * 128].astype(bf16)
         core_copy(g).start()
-        return 0
-
-    def keep(g, _):
-        product = correlate(core, g)
-        for t in range(group_rows // channels):
-            rows = pl.ds(pl.multiple_of(g * group_rows + t * channels, 32), channels)
-            own[rows, :] = product[:, t * 128 : (t + 1) * 128]
-        return 0
-
-    def join(g, _):
-        core_copy(g).wait_recv()
-        rows = pl.ds(pl.multiple_of(g * group_rows, 32), group_rows)
-        total = own[rows, :] + from_core[rows, :].astype(f32)
-        own[rows, :] = total
-        summed[rows, :] = total.astype(bf16)
-        return 0
-
-    lax.fori_loop(0, GROUPS, give, 0)
-    lax.fori_loop(0, GROUPS, keep, 0)
-    lax.fori_loop(0, GROUPS, join, 0)
-
-    def piece_rows(p):
-        return pl.ds(pl.multiple_of(p * piece, piece), piece)
-
-    def plane_copy(source, target):
-        return remote(
-            summed.at[piece_rows(target), :], arrived.at[source], sem_plane, source, target,
-            (target * 2 + core, smp),
-        )
-
-    def loop(start, stop, act_on):
-        def run(i, _):
-            act_on(i)
-            return 0
-
-        lax.fori_loop(start, stop, run, 0)
-
-    loop(1, nj, lambda i: plane_copy(chip, plane(i)).start())
+
+    def keep(which, g):
+        product = correlate(which, g)
+        for t in range(tiles):
+            own[tile_rows(g, t), :] = product[:, t * 128 : (t + 1) * 128]
+
+    def join():
+        done = 0
+        for p in range(nj):
+            while done < GROUPS and done * group_rows < (p + 1) * piece:
+                core_copy(done).wait_recv()
+                done += 1
+            rows = pl.ds(p * piece, piece)
+            total = own[rows, :] + from_core[rows, :].astype(f32)
+            own[rows, :] = total
+            summed[p, 0:piece, :] = total.astype(bf16)
+            summed[p, piece:, :] = total[:quarter].astype(bf16)
+
+    for which in range(2):
+
+        @pl.when(other == which)
+        def _():
+            loop(0, GROUPS, functools.partial(give, which))
+
+    for which in range(2):
+
+        @pl.when(core == which)
+        def _():
+            loop(0, GROUPS, functools.partial(keep, which))
+
+    join()
+
+    def quarter_rows(q):
+        return pl.ds(pl.multiple_of(q * quarter, 8), quarter)
+
+    starts = (far, near)
+
+    def plane_copy(part, source, target):
+        rows = pl.ds(pl.multiple_of(starts[part] * quarter, 8), some)
+        return pltpu.make_async_remote_copy(
+            src_ref=summed.at[target, rows, :], dst_ref=arrived.at[part, source],
+            send_sem=sem_plane.at[0, part, target], recv_sem=sem_plane.at[1, part, source],
+            device_id=(target * 2 + core, smp), device_id_type=MESH,
+        )
+
+    for part in range(2):
+        loop(1, nj, lambda i: plane_copy(part, chip, plane(i)).start())
 
     arrive_faces(faces_c)
     turned_halo_c = nt(eye(halo_c.shape[1], bf16)[:both], halo_c[...]).astype(bf16)
@@ -273,25 +319,61 @@
         return forth, back
 
     forth, back = lax.fori_loop(0, OFFSETS // UNROLL, second_pass, (zeros, zeros))
-    out_field[...] = (live_f * forth).astype(bf16)
-    input_grad[...] = (live_f * back).astype(bf16)
-
-    z_part[...] = own[piece_rows(chip), :]
-
-    def add_piece(i):
-        source = plane(i)
-        plane_copy(source, source).wait_recv()
-        z_part[...] += arrived[source].astype(f32)
-
-    loop(1, nj, add_piece)
+    results[0] = (live_f * forth).astype(bf16)
+    results[1] = (live_f * back).astype(bf16)
+    keeps = [
+        pltpu.make_async_copy(results.at[0], out_field, sem_out.at[0]),
+        pltpu.make_async_copy(results.at[1], input_grad, sem_out.at[1]),
+    ]
+    for copy in keeps:
+        copy.start()
+
+    def z_copy(source, target, rows):
+        return remote(z_part.at[rows, :], z_in.at[source], sem_z, source, target, (blk, target))
+
+    def z_sends(part, act_on):
+        def run(k):
+            target = lax.rem(starts[part] * (nz // 4) + k, nz)
+            rows = pl.ds(pl.multiple_of(part * some + k * sliver, 8), sliver)
+
+            if part == 0:
+                act_on(target, rows)
+            else:
+
+                @pl.when(target != smp)
+                def _():
+                    act_on(target, rows)
+
+        loop(0, nz // 2, run)
+
+    base = pl.multiple_of(chip * piece, piece)
+    for part in range(2):
+        for k in range(2):
+            first_row = base + lax.rem(starts[part] + k, 4) * quarter
+            z_part[part * some + k * quarter : part * some + (k + 1) * quarter, :] = own[
+                pl.ds(pl.multiple_of(first_row, 8), quarter), :
+            ]
+
+        def add_piece(i):
+            source = plane(i)
+            plane_copy(part, source, source).wait_recv()
+            z_part[part * some : (part + 1) * some, :] += arrived[part, source].astype(f32)
+
+        loop(1, nj, add_piece)
+        z_sends(part, lambda target, rows: z_copy(smp, target, rows).start())
+
+    place_here = lax.rem(smp + nz - near * (nz // 4), nz)
+    total = z_part[pl.ds(pl.multiple_of(some + place_here * sliver, 8), sliver), :]
+
+    def add_sliver(i, running):
+        source = along(i)
+        z_copy(source, source, pl.ds(0, sliver)).wait_recv()
+        return running + z_in[source]
+
+    total = lax.fori_loop(1, nz, add_sliver, total)
 
     def sliver_rows(s):
         return pl.ds(pl.multiple_of(s * sliver, 8), sliver)
-
-    def z_copy(source, target):
-        return remote(
-            z_part.at[sliver_rows(target), :], z_in.at[source], sem_z, source, target, (blk, target)
-        )
 
     def zg_copy(source, target):
         return remote(
@@ -299,60 +381,137 @@
             (blk, target),
         )
 
-    loop(1, nz, lambda i: z_copy(smp, along(i)).start())
-    z_in[smp] = z_part[sliver_rows(smp), :]
-    loop(1, nz, lambda i: z_copy(along(i), along(i)).wait_recv())
-    total = z_in[0]
-    for s in range(1, nz):
-        total = total + z_in[s]
     z_out[sliver_rows(smp), :] = total
-    loop(1, nz, lambda i: zg_copy(smp, along(i)).start())
-    loop(1, nz, lambda i: zg_copy(along(i), along(i)).wait_recv())
-
-    def gather_copy(source, target):
-        here = gathered.at[core, piece_rows(source), :]
-        return remote(here, here, sem_gather, source, target, (target * 2 + core, smp))
-
-    def forward_copy(which, p):
-        here = gathered.at[which, piece_rows(p), :]
-        return remote(here, here, sem_forward, p, p, partner)
-
-    gathered[core, piece_rows(chip), :] = z_out[...].astype(bf16)
-    loop(1, nj, lambda i: gather_copy(chip, plane(i)).start())
-    forward_copy(core, chip).start()
-
-    def hand_on(i):
-        source = plane(i)
-        gather_copy(source, source).wait_recv()
-        forward_copy(core, source).start()
-
-    loop(1, nj, hand_on)
-    loop(0, nj, lambda p: forward_copy(other, p).wait_recv())
+    loop(0, nz - 1, lambda i: zg_copy(smp, along(lax.rem(i + nz // 2 - 1, nz - 1) + 1)).start())
+
+    def gather_copy(part, source, target):
+        return pltpu.make_async_remote_copy(
+            src_ref=spreading.at[chip, part], dst_ref=spreading.at[source, part],
+            send_sem=sem_gather.at[0, part, target], recv_sem=sem_gather.at[1, part, source],
+            device_id=(target * 2 + core, smp), device_id_type=MESH,
+        )
+
+    def keep_copy(part, p):
+        return pltpu.make_async_copy(spreading.at[p, part], gathered.at[core, p, part], sem_keep.at[part, p])
+
+    def forward_copy(which, part, p):
+        return pltpu.make_async_remote_copy(
+            src_ref=spreading.at[p, part], dst_ref=gathered.at[which, p, part],
+            send_sem=sem_forward.at[0, part, p], recv_sem=sem_forward.at[1, part, p],
+            device_id=partner, device_id_type=MESH,
+        )
+
+    def store(part, p):
+        keep_copy(part, p).start()
+        forward_copy(core, part, p).start()
+
+    for part, start in enumerate((near, far)):
+
+        def sliver_here(k):
+            source = lax.rem(start * (nz // 4) + k, nz)
+            if part == 0:
+                pl.when(source != smp)(lambda: zg_copy(source, source).wait_recv())
+            else:
+                zg_copy(source, source).wait_recv()
+
+        loop(0, nz // 2, sliver_here)
+        for k in range(2):
+            spreading[chip, part, k * quarter : (k + 1) * quarter, :] = z_out[
+                quarter_rows(lax.rem(start + k, 4)), :
+            ].astype(bf16)
+        loop(1, nj, lambda i: gather_copy(part, chip, plane(i)).start())
+        store(part, chip)
+
+    for part in range(2):
+
+        def hand_on(i):
+            source = plane(i)
+            gather_copy(part, source, source).wait_recv()
+            store(part, source)
+
+        loop(1, nj, hand_on)
 
     finish_faces(faces_a)
     finish_faces(faces_c)
     loop(0, GROUPS, lambda g: core_copy(g).wait_send())
-    loop(1, nj, lambda i: plane_copy(chip, plane(i)).wait_send())
-    loop(1, nz, lambda i: z_copy(smp, along(i)).wait_send())
+    for part in range(2):
+        loop(1, nj, lambda i: plane_copy(part, chip, plane(i)).wait_send())
+        z_sends(part, lambda target, rows: z_copy(smp, target, rows).wait_send())
+        loop(1, nj, lambda i: gather_copy(part, chip, plane(i)).wait_send())
     loop(1, nz, lambda i: zg_copy(smp, along(i)).wait_send())
-    loop(1, nj, lambda i: gather_copy(chip, plane(i)).wait_send())
-    loop(0, nj, lambda p: forward_copy(core, p).wait_send())
-
-
-def unpack_kernel(scale, sums, field_in, grad_in, first, second, field_out, grad_out):
-    channels = first.shape[1]
-    field_out[0] = field_in[...]
-    grad_out[0] = grad_in[...]
-    unit = eye(channels, jnp.bfloat16)
+    for copy in keeps:
+        copy.wait()
+    for part in range(2):
+
+        def settle(p):
+            keep_copy(part, p).wait()
+            forward_copy(core, part, p).wait_send()
+            forward_copy(other, part, p).wait_recv()
+
+        loop(0, nj, settle)
+
+
+def unpack_kernel(
+    nj, nz, scale, field_in, grad_in, gathered, first, second, field_out, grad_out,
+    fields, stage, wide_sums, sem_field, sem_in, sem_out,
+):
+    channels, offsets = first.shape[1], first.shape[0]
+    half_rows = stage.shape[1]
+    quarter = half_rows // nj // 4
+    group_rows = GROUP * channels * channels // 128
     tiles = GROUP * channels // 128
-    for which, out in enumerate((first, second)):
-        wide = jnp.concatenate(
-            [sums[which, t * channels : (t + 1) * channels, :] for t in range(tiles)], axis=1
-        )
-        for k in range(GROUP):
-            block = wide[:, k * channels : (k + 1) * channels]
-            block = nt(unit, block) if which else block.astype(jnp.float32)
-            out[k] = block * scale
+    run = 32
+    near = lax.rem(far_quarter(lax.axis_index("smp"), nz) + 2, 4)
+    turned = [pl.multiple_of(lax.rem(q + 4 - near, 4) * quarter, 8) for q in range(4)]
+
+    def load(which, k):
+        rows = pl.ds(k * (half_rows // 4), half_rows // 4)
+        return pltpu.make_async_copy(gathered.at[which, rows], stage.at[which, rows], sem_in.at[which, k])
+
+    def save(which, g):
+        some = pl.ds(g * GROUP, min(GROUP, offsets - g * GROUP))
+        return pltpu.make_async_copy(
+            wide_sums.at[which, some], (first, second)[which].at[some], sem_out.at[which, g]
+        )
+
+    loads = [pltpu.make_async_copy(x, fields.at[i], sem_field.at[0, i]) for i, x in enumerate((field_in, grad_in))]
+    saves = [
+        pltpu.make_async_copy(fields.at[i], x.at[0], sem_field.at[1, i]) for i, x in enumerate((field_out, grad_out))
+    ]
+    for which in range(2):
+        for k in range(4):
+            load(which, k).start()
+    for copy in loads:
+        copy.start()
+    for which in range(2):
+        here = 0
+        for g in range(GROUPS):
+            while here < 4 and here * (half_rows // 4) < (g + 1) * group_rows:
+                load(which, here).wait()
+                here += 1
+
+            def part_of(row):
+                first_row = row - row % (quarter * 4) + turned[row // quarter % 4] + row % quarter
+                return stage[which, pl.ds(pl.multiple_of(first_row, 8), run), :].astype(jnp.float32)
+
+            parts = [part_of(g * group_rows + n) for n in range(0, group_rows, run)]
+            step = channels // run
+            wide = jnp.concatenate(
+                [jnp.concatenate(parts[t * step : (t + 1) * step], axis=0) for t in range(tiles)], axis=1
+            )
+            wide = wide * scale
+            for k in range(GROUP):
+                wide_sums[which, g * GROUP + k] = wide[:, k * channels : (k + 1) * channels]
+            save(which, g).start()
+    for copy in loads:
+        copy.wait()
+    for copy in saves:
+        copy.start()
+    for which in range(2):
+        for g in range(GROUPS):
+            save(which, g).wait()
+    for copy in saves:
+        copy.wait()
 
 
 def body(nb, nz, features, active, neighbour_rows, send_rows, first_weight, second_weight, cotangent):
@@ -364,7 +523,10 @@
     half_rows = 2048
     piece = half_rows // nj
     bf16, f32 = jnp.bfloat16, jnp.float32
-    vmem = pl.BlockSpec(memory_space=pltpu.VMEM)
+    anywhere = pl.BlockSpec(memory_space=pl.ANY)
+    slots = lax.axis_size("smp") * features.shape[0] * nb * voxels
+    table = jnp.transpose(neighbour_rows, (1, 0, 2))
+    operands = (features, active, table, send_rows, first_weight, second_weight, cotangent)
     dma = pltpu.SemaphoreType.DMA
     wide = 256
     out_field, input_grad, gathered = pl.pallas_call(
@@ -372,11 +534,14 @@
         out_shape=[
             jax.ShapeDtypeStruct((channels, voxels), bf16),
             jax.ShapeDtypeStruct((channels, voxels), bf16),
-            jax.ShapeDtypeStruct((2, half_rows, 128), bf16),
+            jax.ShapeDtypeStruct((2, nj, 2, piece // 2, 128), bf16),
         ],
-        in_specs=[vmem] * 7,
-        out_specs=[vmem] * 3,
+        in_specs=[anywhere] * 7,
+        out_specs=[anywhere] * 3,
         scratch_shapes=[
+            *(pltpu.VMEM(x.shape, x.dtype) for x in operands),
+            pltpu.VMEM((2, channels, voxels), bf16),
+            pltpu.VMEM((nj, 2, piece // 2, 128), bf16),
             pltpu.VMEM((both, voxels), bf16),
             pltpu.VMEM((8 * per_list, voxels), bf16),
             pltpu.VMEM((8 * per_list, wide), bf16),
@@ -391,44 +556,47 @@
             pltpu.VMEM((half_rows, 128), bf16),
             pltpu.VMEM((half_rows, 128), f32),
             pltpu.VMEM((half_rows, 128), bf16),
-            pltpu.VMEM((half_rows, 128), bf16),
-            pltpu.VMEM((nj, piece, 128), bf16),
+            pltpu.VMEM((nj, piece + piece // 4, 128), bf16),
+            pltpu.VMEM((2, nj, piece // 2, 128), bf16),
             pltpu.VMEM((piece, 128), f32),
             pltpu.VMEM((nz, piece // nz, 128), f32),
             pltpu.VMEM((piece, 128), f32),
+            dma((7,)),
+            dma((2,)),
             dma((2, 8)),
             dma((2, 8)),
             dma((2, GROUPS)),
-            dma((2, nj)),
+            dma((2, 2, nj)),
             dma((2, nz)),
             dma((2, nz)),
+            dma((2, 2, nj)),
             dma((2, nj)),
-            dma((2, nj)),
+            dma((2, 2, nj)),
         ],
         compiler_params=pltpu.CompilerParams(
-            collective_id=0, has_side_effects=True, vmem_limit_bytes=40 * 2**20
+            collective_id=0, has_side_effects=True, vmem_limit_bytes=56 * 2**20
         ),
         name="halo_conv_and_sum",
-    )(features, active, neighbour_rows, send_rows, first_weight, second_weight, cotangent)
-
-    slots = lax.axis_size("smp") * features.shape[0] * nb * voxels
-    group_rows = GROUP * channels * channels // 128
-    whole = pl.BlockSpec((channels, voxels), lambda g: (0, 0))
-    whole_out = pl.BlockSpec((1, channels, voxels), lambda g: (0, 0, 0))
-    grads = pl.BlockSpec((GROUP, channels, channels), lambda g: (g, 0, 0))
+    )(*operands)
+
+    grad = jax.ShapeDtypeStruct((OFFSETS, channels, channels), f32)
+    field = jax.ShapeDtypeStruct((1, channels, voxels), bf16)
     first_grad, second_grad, out_field, input_grad = pl.pallas_call(
-        functools.partial(unpack_kernel, 1.0 / slots**0.5),
-        grid=(GROUPS,),
-        out_shape=[
-            jax.ShapeDtypeStruct((OFFSETS, channels, channels), f32),
-            jax.ShapeDtypeStruct((OFFSETS, channels, channels), f32),
-            jax.ShapeDtypeStruct((1, channels, voxels), bf16),
-            jax.ShapeDtypeStruct((1, channels, voxels), bf16),
+        functools.partial(unpack_kernel, nj, nz, 1.0 / slots**0.5),
+        out_shape=[grad, grad, field, field],
+        in_specs=[anywhere] * 3,
+        out_specs=[anywhere] * 4,
+        scratch_shapes=[
+            pltpu.VMEM((2, channels, voxels), bf16),
+            pltpu.VMEM((2, half_rows, 128), bf16),
+            pltpu.VMEM((2, GROUP * GROUPS, channels, channels), f32),
+            dma((2, 2)),
+            dma((2, 4)),
+            dma((2, GROUPS)),
         ],
-        in_specs=[pl.BlockSpec((2, group_rows, 128), lambda g: (0, g, 0)), whole, whole],
-        out_specs=[grads, grads, whole_out, whole_out],
+        compiler_params=pltpu.CompilerParams(vmem_limit_bytes=56 * 2**20),
         name="unpack",
-    )(gathered, out_field, input_grad)
+    )(out_field, input_grad, gathered.reshape(2, half_rows, 128))
     return out_field, input_grad, first_grad, second_grad
 
 

time: 82.5 us -> 67.4 us (0.82)
  local copies, waits for them, and re-layouts: 8.1 us -> 0 us
  Pallas kernels: 73.2 us -> 66.6 us
    unnamed x19 -> x0, local copies, waits for them, and re-layouts: 8.1 us -> none
    pallas_call x1, Pallas kernels: 67.3 us -> 63.3 us  [body(): pl.pallas_call(functools.partial(main_kernel, nb, nz), out_shape=[jax.Sha...]
    pallas_call x1, Pallas kernels: 5.92 us -> 3.27 us  [body(): pl.pallas_call(functools.partial(unpack_kernel, nj, nz, 1.0 / slots ** 0....]
where the time goes in v2:
time: 67.4 us; the launch traced here: 67.3 us
  Pallas kernels  66.6 us (99%)
    pallas_call x1, Pallas kernels, body(): pl.pallas_call(functools.partial(main_kernel, nb, nz), out_shape=[jax.Sha...  63.3 us
    pallas_call x1, Pallas kernels, body(): pl.pallas_call(functools.partial(unpack_kernel, nj, nz, 1.0 / slots ** 0....  3.27 us

profile of v2, /device:TPU:1, one launch (start us, length us, event | category | flops | bytes accessed | tf_op | source)
XLA Modules:
  0.0 67.3 jit_solution(12482346778251945210)
XLA Ops:
  0.6 63.3 %halo_conv_and_sum.1 = (bf16[96,256]{1,0:T(8,128)(2,1)}, bf16[96,256]{1,0:T(8,128)(2,1)}, bf16[2,16,2,64,128]{4,3,2,1,0:T(8,128)(2,1)}) custom-call(bf16[1,96,256]{2,1,0:T(8,128)(2,1)} %feat_in.1, s32[1,256]{1,0:T(1,128)} %act_in.1, s32[27,1,256]{2,1,0:T(1,128)} %bitcast.3, s32[1,1,8,32]{3,2,1,0:T(8,128)} %lists_in.1, bf16[27,96,96]{2,1,0:T(8,128)(2,1)} %w1_in.1, ...), custom_call_target="tpu_custom_call" | custom-call | tf_op jit(solution)/shard_map/halo_conv_and_sum/pallas_call | solution.py:532
  64.0 3.3 %unpack.1 = (f32[27,96,96]{2,1,0:T(8,128)}, f32[27,96,96]{2,1,0:T(8,128)}, bf16[1,96,256]{2,1,0:T(8,128)(2,1)}, bf16[1,96,256]{2,1,0:T(8,128)(2,1)}) custom-call(bf16[96,256]{1,0:T(8,128)(2,1)} %get-tuple-element.11.field_in, bf16[96,256]{1,0:T(8,128)(2,1)} %get-tuple-element.12.grad_in, bf16[2,2048,128]{2,1,0:T(8,128)(2,1)} %bitcast.2), custom_call_target="tpu_custom_call" | custom-call | tf_op jit(solution)/shard_map/unpack/pallas_call | solution.py:584

commit v3 on v2

--- a/solution.py
+++ b/solution.py
@@ -15,7 +15,7 @@
 GROUP = 4
 GROUPS = 7
 CORNER = 16
-UNROLL = 3
+UNROLL = 9
 
 
 def nn(a, b):
@@ -50,7 +50,7 @@
     field, pick, sent_a, halo_a, sent_c, halo_c,
     local_hot, halo_hot, turned, picked, sides,
     to_core, own, from_core, summed, arrived, z_part, z_in, z_out,
-    sem_in, sem_out, sem_a, sem_c, sem_core, sem_plane, sem_z, sem_zg, sem_gather, sem_keep, sem_forward,
+    heard, sem_in, sem_out, sem_a, sem_c, sem_core, sem_plane, sem_z, sem_zg, sem_gather, sem_keep, sem_forward,
 ):
     bf16, f32 = jnp.bfloat16, jnp.float32
     channels, voxels = feat.shape[1], feat.shape[2]
@@ -116,8 +116,17 @@
         pl.semaphore_signal(barrier, inc=1, device_id=(blk, along(i)), device_id_type=MESH)
         return 0
 
+    def tell(step):
+        for i in (1 << step, nz - (1 << step)):
+            pl.semaphore_signal(heard.at[step], inc=1, device_id=(blk, along(i)), device_id_type=MESH)
+
+    def hear(step):
+        pl.semaphore_wait(heard.at[step], 2)
+
+    rounds = max(nz // 4, 1).bit_length()
     lax.fori_loop(1, nb, greet_blk, 0)
-    lax.fori_loop(1, nz, greet_smp, 0)
+    for i in (1, nz - 1):
+        greet_smp(i, 0)
 
     for load in loads[:4]:
         load.wait()
@@ -170,8 +179,9 @@
     faces_c = face_copies(sent_c, halo_c, sem_c)
     sent_a[:, 0:both] = nt(pick[...], field[...]).astype(bf16)
     sent_a[:, both:] = jnp.zeros((8 * per_list, sent_a.shape[1] - both), bf16)
-    pl.semaphore_wait(barrier, (nb - 1) + (nz - 1))
+    pl.semaphore_wait(barrier, (nb - 1) + 2)
     start_faces(faces_a)
+    tell(0)
 
     for load in loads[4:]:
         load.wait()
@@ -208,6 +218,11 @@
     own[GROUPS * group_rows :, :] = jnp.zeros((rest, 128), f32)
     from_core[GROUPS * group_rows :, :] = jnp.zeros((rest, 128), bf16)
 
+    for step in range(1, rounds):
+        hear(step - 1)
+        tell(step)
+        if step == 1:
+            break
     arrive_faces(faces_a)
     turned_halo = nt(eye(halo_a.shape[1], bf16)[:both], halo_a[...]).astype(bf16)
     zeros = jnp.zeros((channels, voxels), f32)
@@ -238,6 +253,9 @@
     sent_c[:, 0:both] = nt(pick[...], field[...]).astype(bf16)
     sent_c[:, both:] = jnp.zeros((8 * per_list, sent_c.shape[1] - both), bf16)
     start_faces(faces_c)
+    for step in range(2, rounds):
+        hear(step - 1)
+        tell(step)
 
     def core_copy(g):
         rows = pl.ds(pl.multiple_of(g * group_rows, 32), group_rows)
@@ -278,15 +296,12 @@
 
     for which in range(2):
 
-        @pl.when(other == which)
-        def _():
-            loop(0, GROUPS, functools.partial(give, which))
-
-    for which in range(2):
-
         @pl.when(core == which)
         def _():
-            loop(0, GROUPS, functools.partial(keep, which))
+            for g in range(GROUPS):
+                give(1 - which, g)
+            for g in range(GROUPS):
+                keep(which, g)
 
     join()
 
@@ -305,6 +320,7 @@
 
     for part in range(2):
         loop(1, nj, lambda i: plane_copy(part, chip, plane(i)).start())
+    hear(rounds - 1)
 
     arrive_faces(faces_c)
     turned_halo_c = nt(eye(halo_c.shape[1], bf16)[:both], halo_c[...]).astype(bf16)
@@ -561,6 +577,7 @@
             pltpu.VMEM((piece, 128), f32),
             pltpu.VMEM((nz, piece // nz, 128), f32),
             pltpu.VMEM((piece, 128), f32),
+            pltpu.SemaphoreType.REGULAR((max(nz // 4, 1).bit_length(),)),
             dma((7,)),
             dma((2,)),
             dma((2, 8)),

time: 67.4 us -> 61.2 us (0.908)
  Pallas kernels: 66.6 us -> 60.4 us
    pallas_call x1, Pallas kernels: 63.3 us -> 57.1 us  [body(): pl.pallas_call(functools.partial(main_kernel, nb, nz), out_shape=[jax.Sha...]
where the time goes in v3:
time: 61.2 us; the launch traced here: 61 us
  Pallas kernels  60.4 us (99%)
  between operations  0.64 us (1%)
    pallas_call x1, Pallas kernels, body(): pl.pallas_call(functools.partial(main_kernel, nb, nz), out_shape=[jax.Sha...  57.1 us
    pallas_call x1, Pallas kernels, body(): pl.pallas_call(functools.partial(unpack_kernel, nj, nz, 1.0 / slots ** 0....  3.27 us

profile of v3, /device:TPU:1, one launch (start us, length us, event | category | flops | bytes accessed | tf_op | source)
XLA Modules:
  0.0 61.0 jit_solution(16373837903653002180)
XLA Ops:
  0.6 57.1 %halo_conv_and_sum.1 = (bf16[96,256]{1,0:T(8,128)(2,1)}, bf16[96,256]{1,0:T(8,128)(2,1)}, bf16[2,16,2,64,128]{4,3,2,1,0:T(8,128)(2,1)}) custom-call(bf16[1,96,256]{2,1,0:T(8,128)(2,1)} %feat_in.1, s32[1,256]{1,0:T(1,128)} %act_in.1, s32[27,1,256]{2,1,0:T(1,128)} %bitcast.3, s32[1,1,8,32]{3,2,1,0:T(8,128)} %lists_in.1, bf16[27,96,96]{2,1,0:T(8,128)(2,1)} %w1_in.1, ...), custom_call_target="tpu_custom_call" | custom-call | tf_op jit(solution)/shard_map/halo_conv_and_sum/pallas_call | solution.py:548
  57.7 3.3 %unpack.1 = (f32[27,96,96]{2,1,0:T(8,128)}, f32[27,96,96]{2,1,0:T(8,128)}, bf16[1,96,256]{2,1,0:T(8,128)(2,1)}, bf16[1,96,256]{2,1,0:T(8,128)(2,1)}) custom-call(bf16[96,256]{1,0:T(8,128)(2,1)} %get-tuple-element.11.field_in, bf16[96,256]{1,0:T(8,128)(2,1)} %get-tuple-element.12.grad_in, bf16[2,2048,128]{2,1,0:T(8,128)(2,1)} %bitcast.2), custom_call_target="tpu_custom_call" | custom-call | tf_op jit(solution)/shard_map/unpack/pallas_call | solution.py:601

commit v4 on v3

--- a/solution.py
+++ b/solution.py
@@ -48,7 +48,7 @@
     out_field, input_grad, gathered,
     feat, act, nbr, lists, w1, w2, cot, results, spreading,
     field, pick, sent_a, halo_a, sent_c, halo_c,
-    local_hot, halo_hot, turned, picked, sides,
+    local_hot, halo_hot, turned, side_by_side, picked, sides,
     to_core, own, from_core, summed, arrived, z_part, z_in, z_out,
     heard, sem_in, sem_out, sem_a, sem_c, sem_core, sem_plane, sem_z, sem_zg, sem_gather, sem_keep, sem_forward,
 ):
@@ -94,6 +94,16 @@
             device_id=device, device_id_type=MESH,
         )
 
+    halo_a[...] = jnp.zeros_like(halo_a)
+    halo_c[...] = jnp.zeros_like(halo_c)
+    barrier = pltpu.get_barrier_semaphore()
+    in_range = [(blk + delta >= 0) & (blk + delta < nb) for delta in DELTAS]
+
+    def greet(device):
+        pl.semaphore_signal(barrier, inc=1, device_id=device, device_id_type=MESH)
+
+    for delta, there in zip(DELTAS, in_range):
+        pl.when(there)(functools.partial(greet, (jnp.clip(blk + delta, 0, nb - 1), smp)))
     loads = [
         pltpu.make_async_copy(src, dst, sem_in.at[i])
         for i, (src, dst) in enumerate(
@@ -102,31 +112,32 @@
     ]
     for load in loads:
         load.start()
-    halo_a[...] = jnp.zeros_like(halo_a)
-    halo_c[...] = jnp.zeros_like(halo_c)
-    barrier = pltpu.get_barrier_semaphore()
-
-    def greet_blk(i, _):
-        pl.semaphore_signal(
-            barrier, inc=1, device_id=(lax.rem(blk + i, nb), smp), device_id_type=MESH
-        )
-        return 0
-
-    def greet_smp(i, _):
-        pl.semaphore_signal(barrier, inc=1, device_id=(blk, along(i)), device_id_type=MESH)
-        return 0
+
+    across = min(4, nj)
+    row, place_in_row = lax.div(chip, across), lax.rem(chip, across)
+    beside = [row * across + lax.rem(place_in_row + step, across) for step in (1, across - 1)]
+    if nj > across:
+        beside += [lax.rem(chip + step, nj) for step in (across, nj - across)]
+    beside = [(p * 2 + core, smp) for p in beside]
+    for device in beside + [(blk, along(1)), (blk, along(nz - 1))]:
+        greet(device)
+    greeted = sum(there.astype(jnp.int32) for there in in_range) + len(beside) + 2
 
     def tell(step):
-        for i in (1 << step, nz - (1 << step)):
-            pl.semaphore_signal(heard.at[step], inc=1, device_id=(blk, along(i)), device_id_type=MESH)
-
-    def hear(step):
-        pl.semaphore_wait(heard.at[step], 2)
+        for device in beside:
+            pl.semaphore_signal(heard.at[0, step], inc=1, device_id=device, device_id_type=MESH)
+        if step < rounds:
+            for i in (1 << step, nz - (1 << step)):
+                pl.semaphore_signal(heard.at[1, step], inc=1, device_id=(blk, along(i)), device_id_type=MESH)
+
+    def hear_plane(step):
+        pl.semaphore_wait(heard.at[0, step], len(beside))
+
+    def hear_samples(step):
+        if step < rounds:
+            pl.semaphore_wait(heard.at[1, step], 2)
 
     rounds = max(nz // 4, 1).bit_length()
-    lax.fori_loop(1, nb, greet_blk, 0)
-    for i in (1, nz - 1):
-        greet_smp(i, 0)
 
     for load in loads[:4]:
         load.wait()
@@ -179,7 +190,7 @@
     faces_c = face_copies(sent_c, halo_c, sem_c)
     sent_a[:, 0:both] = nt(pick[...], field[...]).astype(bf16)
     sent_a[:, both:] = jnp.zeros((8 * per_list, sent_a.shape[1] - both), bf16)
-    pl.semaphore_wait(barrier, (nb - 1) + 2)
+    pl.semaphore_wait(barrier, greeted)
     start_faces(faces_a)
     tell(0)
 
@@ -207,41 +218,46 @@
             got = nn(field[...], hot).astype(bf16)
             picked[0, at(o), :] = got[:channels]
             picked[1, at(OFFSETS - 1 - o), :] = got[channels:]
-            turned[0, o] = nt(unit, w1[o]).astype(bf16)
-            turned[1, o] = nt(unit, w2[o]).astype(bf16)
+            turned[o] = nt(unit, w1[o]).astype(bf16)
         return 0
 
     lax.fori_loop(0, OFFSETS // UNROLL, prepare, 0)
+    blank = jnp.zeros((channels, channels), bf16)
+    for g in range(GROUPS):
+        lanes = pl.ds(g * GROUP * channels, GROUP * channels)
+        group = range(g * GROUP, (g + 1) * GROUP)
+        side_by_side[0, :, lanes] = jnp.concatenate([w1[o] if o < OFFSETS else blank for o in group], axis=1)
+        side_by_side[1, :, lanes] = jnp.concatenate(
+            [nt(unit, w2[o]) if o < OFFSETS else blank.astype(f32) for o in group], axis=1
+        ).astype(bf16)
     tail = picked.shape[1] - OFFSETS * channels
     picked[:, OFFSETS * channels :, :] = jnp.zeros((2, tail, voxels), bf16)
     rest = half_rows - GROUPS * group_rows
     own[GROUPS * group_rows :, :] = jnp.zeros((rest, 128), f32)
     from_core[GROUPS * group_rows :, :] = jnp.zeros((rest, 128), bf16)
 
-    for step in range(1, rounds):
-        hear(step - 1)
-        tell(step)
-        if step == 1:
-            break
+    hear_plane(0)
+    hear_samples(0)
+    tell(1)
     arrive_faces(faces_a)
     turned_halo = nt(eye(halo_a.shape[1], bf16)[:both], halo_a[...]).astype(bf16)
     zeros = jnp.zeros((channels, voxels), f32)
 
-    def first_pass(step, sums):
-        forth, back = sums
+    def first_pass(step, _):
         for u in range(UNROLL):
             o = step * UNROLL + u
             mirror = OFFSETS - 1 - o
             got = nn(turned_halo, halo_hot[o]).astype(bf16)
-            mine = picked[0, at(o), :] + got[:channels]
-            theirs = picked[1, at(mirror), :] + got[channels:]
-            picked[0, at(o), :] = mine
-            picked[1, at(mirror), :] = theirs
-            forth = forth + nn(w1[o], mine)
-            back = back + nn(turned[1, mirror], theirs)
-        return forth, back
-
-    forth, back = lax.fori_loop(0, OFFSETS // UNROLL, first_pass, (zeros, zeros))
+            picked[0, at(o), :] += got[:channels]
+            picked[1, at(mirror), :] += got[channels:]
+        return 0
+
+    lax.fori_loop(0, OFFSETS // UNROLL, first_pass, 0)
+    hear_plane(1)
+    hear_samples(1)
+    tell(2)
+    forth = nn(side_by_side[0], picked[0])
+    back = nn(side_by_side[1], picked[1])
     pre = live_f * forth
     gate = 1.0 / (1.0 + jnp.exp(-pre))
     hidden = (live_f * (pre * gate)).astype(bf16)
@@ -253,9 +269,6 @@
     sent_c[:, 0:both] = nt(pick[...], field[...]).astype(bf16)
     sent_c[:, both:] = jnp.zeros((8 * per_list, sent_c.shape[1] - both), bf16)
     start_faces(faces_c)
-    for step in range(2, rounds):
-        hear(step - 1)
-        tell(step)
 
     def core_copy(g):
         rows = pl.ds(pl.multiple_of(g * group_rows, 32), group_rows)
@@ -318,9 +331,44 @@
             device_id=(target * 2 + core, smp), device_id_type=MESH,
         )
 
+    hear_plane(2)
     for part in range(2):
         loop(1, nj, lambda i: plane_copy(part, chip, plane(i)).start())
-    hear(rounds - 1)
+
+    def z_copy(source, target, rows):
+        return remote(z_part.at[rows, :], z_in.at[source], sem_z, source, target, (blk, target))
+
+    def z_sends(part, act_on):
+        def run(k):
+            target = lax.rem(starts[part] * (nz // 4) + k, nz)
+            rows = pl.ds(pl.multiple_of(part * some + k * sliver, 8), sliver)
+
+            if part == 0:
+                act_on(target, rows)
+            else:
+
+                @pl.when(target != smp)
+                def _():
+                    act_on(target, rows)
+
+        loop(0, nz // 2, run)
+
+    hear_samples(2)
+    base = pl.multiple_of(chip * piece, piece)
+    for part in range(2):
+        for k in range(2):
+            first_row = base + lax.rem(starts[part] + k, 4) * quarter
+            z_part[part * some + k * quarter : part * some + (k + 1) * quarter, :] = own[
+                pl.ds(pl.multiple_of(first_row, 8), quarter), :
+            ]
+
+        def add_piece(i):
+            source = plane(i)
+            plane_copy(part, source, source).wait_recv()
+            z_part[part * some : (part + 1) * some, :] += arrived[part, source].astype(f32)
+
+        loop(1, nj, add_piece)
+        z_sends(part, lambda target, rows: z_copy(smp, target, rows).start())
 
     arrive_faces(faces_c)
     turned_halo_c = nt(eye(halo_c.shape[1], bf16)[:both], halo_c[...]).astype(bf16)
@@ -331,10 +379,35 @@
             o = step * UNROLL + u
             got = (nn(field[...], local_hot[o]) + nn(turned_halo_c, halo_hot[o])).astype(bf16)
             forth = forth + nn(w2[o], got[:channels])
-            back = back + nn(turned[0, OFFSETS - 1 - o], got[channels:])
+            back = back + nn(turned[OFFSETS - 1 - o], got[channels:])
         return forth, back
 
-    forth, back = lax.fori_loop(0, OFFSETS // UNROLL, second_pass, (zeros, zeros))
+    most = OFFSETS // UNROLL - 1
+    forth, back = lax.fori_loop(0, most, second_pass, (zeros, zeros))
+
+    place_here = lax.rem(smp + nz - near * (nz // 4), nz)
+    total = z_part[pl.ds(pl.multiple_of(some + place_here * sliver, 8), sliver), :]
+
+    def add_sliver(i, running):
+        source = along(i)
+        z_copy(source, source, pl.ds(0, sliver)).wait_recv()
+        return running + z_in[source]
+
+    total = lax.fori_loop(1, nz, add_sliver, total)
+
+    def sliver_rows(s):
+        return pl.ds(pl.multiple_of(s * sliver, 8), sliver)
+
+    def zg_copy(source, target):
+        return remote(
+            z_out.at[sliver_rows(source), :], z_out.at[sliver_rows(source), :], sem_zg, source, target,
+            (blk, target),
+        )
+
+    z_out[sliver_rows(smp), :] = total
+    loop(0, nz - 1, lambda i: zg_copy(smp, along(lax.rem(i + nz // 2 - 1, nz - 1) + 1)).start())
+
+    forth, back = lax.fori_loop(most, OFFSETS // UNROLL, second_pass, (forth, back))
     results[0] = (live_f * forth).astype(bf16)
     results[1] = (live_f * back).astype(bf16)
     keeps = [
@@ -343,62 +416,6 @@
     ]
     for copy in keeps:
         copy.start()
-
-    def z_copy(source, target, rows):
-        return remote(z_part.at[rows, :], z_in.at[source], sem_z, source, target, (blk, target))
-
-    def z_sends(part, act_on):
-        def run(k):
-            target = lax.rem(starts[part] * (nz // 4) + k, nz)
-            rows = pl.ds(pl.multiple_of(part * some + k * sliver, 8), sliver)
-
-            if part == 0:
-                act_on(target, rows)
-            else:
-
-                @pl.when(target != smp)
-                def _():
-                    act_on(target, rows)
-
-        loop(0, nz // 2, run)
-
-    base = pl.multiple_of(chip * piece, piece)
-    for part in range(2):
-        for k in range(2):
-            first_row = base + lax.rem(starts[part] + k, 4) * quarter
-            z_part[part * some + k * quarter : part * some + (k + 1) * quarter, :] = own[
-                pl.ds(pl.multiple_of(first_row, 8), quarter), :
-            ]
-
-        def add_piece(i):
-            source = plane(i)
-            plane_copy(part, source, source).wait_recv()
-            z_part[part * some : (part + 1) * some, :] += arrived[part, source].astype(f32)
-
-        loop(1, nj, add_piece)
-        z_sends(part, lambda target, rows: z_copy(smp, target, rows).start())
-
-    place_here = lax.rem(smp + nz - near * (nz // 4), nz)
-    total = z_part[pl.ds(pl.multiple_of(some + place_here * sliver, 8), sliver), :]
-
-    def add_sliver(i, running):
-        source = along(i)
-        z_copy(source, source, pl.ds(0, sliver)).wait_recv()
-        return running + z_in[source]
-
-    total = lax.fori_loop(1, nz, add_sliver, total)
-
-    def sliver_rows(s):
-        return pl.ds(pl.multiple_of(s * sliver, 8), sliver)
-
-    def zg_copy(source, target):
-        return remote(
-            z_out.at[sliver_rows(source), :], z_out.at[sliver_rows(source), :], sem_zg, source, target,
-            (blk, target),
-        )
-
-    z_out[sliver_rows(smp), :] = total
-    loop(0, nz - 1, lambda i: zg_copy(smp, along(lax.rem(i + nz // 2 - 1, nz - 1) + 1)).start())
 
     def gather_copy(part, source, target):
         return pltpu.make_async_remote_copy(
@@ -566,7 +583,8 @@
             pltpu.VMEM((halo_rows, wide), bf16),
             pltpu.VMEM((OFFSETS, voxels, voxels), bf16),
             pltpu.VMEM((OFFSETS, halo_rows, voxels), bf16),
-            pltpu.VMEM((2, OFFSETS, channels, channels), bf16),
+            pltpu.VMEM((OFFSETS, channels, channels), bf16),
+            pltpu.VMEM((2, channels, GROUP * GROUPS * channels), bf16),
             pltpu.VMEM((2, GROUP * GROUPS * channels, voxels), bf16),
             pltpu.VMEM((2, channels, voxels), bf16),
             pltpu.VMEM((half_rows, 128), bf16),
@@ -577,7 +595,7 @@
             pltpu.VMEM((piece, 128), f32),
             pltpu.VMEM((nz, piece // nz, 128), f32),
             pltpu.VMEM((piece, 128), f32),
-            pltpu.SemaphoreType.REGULAR((max(nz // 4, 1).bit_length(),)),
+            pltpu.SemaphoreType.REGULAR((2, 3)),
             dma((7,)),
             dma((2,)),
             dma((2, 8)),

time: 61.2 us -> 60.2 us (0.984)
  Pallas kernels: 60.4 us -> 59.4 us
    pallas_call x1, Pallas kernels: 57.1 us -> 56.1 us  [body(): pl.pallas_call(functools.partial(main_kernel, nb, nz), out_shape=[jax.Sha...]
where the time goes in v4:
time: 60.2 us; the launch traced here: 60 us
  Pallas kernels  59.4 us (99%)
  between operations  0.64 us (1%)
    pallas_call x1, Pallas kernels, body(): pl.pallas_call(functools.partial(main_kernel, nb, nz), out_shape=[jax.Sha...  56.1 us
    pallas_call x1, Pallas kernels, body(): pl.pallas_call(functools.partial(unpack_kernel, nj, nz, 1.0 / slots ** 0....  3.27 us

profile of v4, /device:TPU:1, one launch (start us, length us, event | category | flops | bytes accessed | tf_op | source)
XLA Modules:
  0.0 60.0 jit_solution(10466728114987472978)
XLA Ops:
  0.6 56.1 %halo_conv_and_sum.1 = (bf16[96,256]{1,0:T(8,128)(2,1)}, bf16[96,256]{1,0:T(8,128)(2,1)}, bf16[2,16,2,64,128]{4,3,2,1,0:T(8,128)(2,1)}) custom-call(bf16[1,96,256]{2,1,0:T(8,128)(2,1)} %feat_in.1, s32[1,256]{1,0:T(1,128)} %act_in.1, s32[27,1,256]{2,1,0:T(1,128)} %bitcast.3, s32[1,1,8,32]{3,2,1,0:T(8,128)} %lists_in.1, bf16[27,96,96]{2,1,0:T(8,128)(2,1)} %w1_in.1, ...), custom_call_target="tpu_custom_call" | custom-call | tf_op jit(solution)/shard_map/halo_conv_and_sum/pallas_call | solution.py:565
  56.8 3.3 %unpack.1 = (f32[27,96,96]{2,1,0:T(8,128)}, f32[27,96,96]{2,1,0:T(8,128)}, bf16[1,96,256]{2,1,0:T(8,128)(2,1)}, bf16[1,96,256]{2,1,0:T(8,128)(2,1)}) custom-call(bf16[96,256]{1,0:T(8,128)(2,1)} %get-tuple-element.11.field_in, bf16[96,256]{1,0:T(8,128)(2,1)} %get-tuple-element.12.grad_in, bf16[2,2048,128]{2,1,0:T(8,128)(2,1)} %bitcast.2), custom_call_target="tpu_custom_call" | custom-call | tf_op jit(solution)/shard_map/unpack/pallas_call | solution.py:619

commit v5 on v4

--- a/solution.py
+++ b/solution.py
@@ -82,8 +82,18 @@
     far = far_quarter(smp, nz)
     near = lax.rem(far + 2, 4)
 
-    def plane(i):
-        return lax.rem(chip + i, nj)
+    across = min(4, nj)
+    row, place_in_row = lax.div(chip, across), lax.rem(chip, across)
+
+    def ring_step(k, n):
+        return jnp.where(k == n - 1, 0, n // 2 + jnp.where(lax.rem(k, 2) == 1, -lax.div(k + 1, 2), lax.div(k, 2)))
+
+    def plane(k):
+        down = lax.rem(row + ring_step(lax.div(k, across), nj // across), nj // across) if nj > across else row
+        return down * across + lax.rem(place_in_row + ring_step(lax.rem(k, across), across), across)
+
+    def plane_back(k):
+        return plane(nj - 2 - k)
 
     def along(i):
         return lax.rem(smp + i, nz)
@@ -113,8 +123,6 @@
     for load in loads:
         load.start()
 
-    across = min(4, nj)
-    row, place_in_row = lax.div(chip, across), lax.rem(chip, across)
     beside = [row * across + lax.rem(place_in_row + step, across) for step in (1, across - 1)]
     if nj > across:
         beside += [lax.rem(chip + step, nj) for step in (across, nj - across)]
@@ -333,7 +341,7 @@
 
     hear_plane(2)
     for part in range(2):
-        loop(1, nj, lambda i: plane_copy(part, chip, plane(i)).start())
+        loop(0, nj - 1, lambda k: plane_copy(part, chip, plane(k)).start())
 
     def z_copy(source, target, rows):
         return remote(z_part.at[rows, :], z_in.at[source], sem_z, source, target, (blk, target))
@@ -362,12 +370,12 @@
                 pl.ds(pl.multiple_of(first_row, 8), quarter), :
             ]
 
-        def add_piece(i):
-            source = plane(i)
+        def add_piece(k):
+            source = plane_back(k)
             plane_copy(part, source, source).wait_recv()
             z_part[part * some : (part + 1) * some, :] += arrived[part, source].astype(f32)
 
-        loop(1, nj, add_piece)
+        loop(0, nj - 1, add_piece)
         z_sends(part, lambda target, rows: z_copy(smp, target, rows).start())
 
     arrive_faces(faces_c)
@@ -405,7 +413,7 @@
         )
 
     z_out[sliver_rows(smp), :] = total
-    loop(0, nz - 1, lambda i: zg_copy(smp, along(lax.rem(i + nz // 2 - 1, nz - 1) + 1)).start())
+    loop(0, nz - 1, lambda k: zg_copy(smp, along(ring_step(k, nz))).start())
 
     forth, back = lax.fori_loop(most, OFFSETS // UNROLL, second_pass, (forth, back))
     results[0] = (live_f * forth).astype(bf16)
@@ -416,6 +424,12 @@
     ]
     for copy in keeps:
         copy.start()
+    finish_faces(faces_a)
+    finish_faces(faces_c)
+    loop(0, GROUPS, lambda g: core_copy(g).wait_send())
+    for part in range(2):
+        loop(0, nj - 1, lambda k: plane_copy(part, chip, plane(k)).wait_send())
+        z_sends(part, lambda target, rows: z_copy(smp, target, rows).wait_send())
 
     def gather_copy(part, source, target):
         return pltpu.make_async_remote_copy(
@@ -425,12 +439,12 @@
         )
 
     def keep_copy(part, p):
-        return pltpu.make_async_copy(spreading.at[p, part], gathered.at[core, p, part], sem_keep.at[part, p])
+        return pltpu.make_async_copy(spreading.at[p, part], gathered.at[core, p, part], sem_keep.at[part])
 
     def forward_copy(which, part, p):
         return pltpu.make_async_remote_copy(
             src_ref=spreading.at[p, part], dst_ref=gathered.at[which, p, part],
-            send_sem=sem_forward.at[0, part, p], recv_sem=sem_forward.at[1, part, p],
+            send_sem=sem_forward.at[0, part], recv_sem=sem_forward.at[1, part],
             device_id=partner, device_id_type=MESH,
         )
 
@@ -452,36 +466,30 @@
             spreading[chip, part, k * quarter : (k + 1) * quarter, :] = z_out[
                 quarter_rows(lax.rem(start + k, 4)), :
             ].astype(bf16)
-        loop(1, nj, lambda i: gather_copy(part, chip, plane(i)).start())
+        loop(0, nj - 1, lambda k: gather_copy(part, chip, plane(k)).start())
         store(part, chip)
 
-    for part in range(2):
-
-        def hand_on(i):
-            source = plane(i)
-            gather_copy(part, source, source).wait_recv()
-            store(part, source)
-
-        loop(1, nj, hand_on)
-
-    finish_faces(faces_a)
-    finish_faces(faces_c)
-    loop(0, GROUPS, lambda g: core_copy(g).wait_send())
-    for part in range(2):
-        loop(1, nj, lambda i: plane_copy(part, chip, plane(i)).wait_send())
-        z_sends(part, lambda target, rows: z_copy(smp, target, rows).wait_send())
-        loop(1, nj, lambda i: gather_copy(part, chip, plane(i)).wait_send())
     loop(1, nz, lambda i: zg_copy(smp, along(i)).wait_send())
     for copy in keeps:
         copy.wait()
     for part in range(2):
 
-        def settle(p):
-            keep_copy(part, p).wait()
-            forward_copy(core, part, p).wait_send()
-            forward_copy(other, part, p).wait_recv()
-
-        loop(0, nj, settle)
+        def hand_on(k):
+            source = plane_back(k)
+            gather_copy(part, source, source).wait_recv()
+            store(part, source)
+
+        loop(0, nj - 1, hand_on)
+        loop(0, nj - 1, lambda k: gather_copy(part, chip, plane(k)).wait_send())
+    for part in range(2):
+        pltpu.make_async_copy(spreading.at[:, part], gathered.at[core, :, part], sem_keep.at[part]).wait()
+        forwarded = pltpu.make_async_remote_copy(
+            src_ref=spreading.at[:, part], dst_ref=gathered.at[other, :, part],
+            send_sem=sem_forward.at[0, part], recv_sem=sem_forward.at[1, part],
+            device_id=partner, device_id_type=MESH,
+        )
+        forwarded.wait_send()
+        forwarded.wait_recv()
 
 
 def unpack_kernel(
@@ -497,8 +505,10 @@
     near = lax.rem(far_quarter(lax.axis_index("smp"), nz) + 2, 4)
     turned = [pl.multiple_of(lax.rem(q + 4 - near, 4) * quarter, 8) for q in range(4)]
 
+    cuts = (0, 3 * half_rows // 16, half_rows // 2, half_rows)
+
     def load(which, k):
-        rows = pl.ds(k * (half_rows // 4), half_rows // 4)
+        rows = pl.ds(cuts[k], cuts[k + 1] - cuts[k])
         return pltpu.make_async_copy(gathered.at[which, rows], stage.at[which, rows], sem_in.at[which, k])
 
     def save(which, g):
@@ -512,14 +522,14 @@
         pltpu.make_async_copy(fields.at[i], x.at[0], sem_field.at[1, i]) for i, x in enumerate((field_out, grad_out))
     ]
     for which in range(2):
-        for k in range(4):
+        for k in range(3):
             load(which, k).start()
     for copy in loads:
         copy.start()
     for which in range(2):
         here = 0
         for g in range(GROUPS):
-            while here < 4 and here * (half_rows // 4) < (g + 1) * group_rows:
+            while here < 3 and cuts[here] < (g + 1) * group_rows:
                 load(which, here).wait()
                 here += 1
 
@@ -605,8 +615,8 @@
             dma((2, nz)),
             dma((2, nz)),
             dma((2, 2, nj)),
-            dma((2, nj)),
-            dma((2, 2, nj)),
+            dma((2,)),
+            dma((2, 2)),
         ],
         compiler_params=pltpu.CompilerParams(
             collective_id=0, has_side_effects=True, vmem_limit_bytes=56 * 2**20
@@ -626,7 +636,7 @@
             pltpu.VMEM((2, half_rows, 128), bf16),
             pltpu.VMEM((2, GROUP * GROUPS, channels, channels), f32),
             dma((2, 2)),
-            dma((2, 4)),
+            dma((2, 3)),
             dma((2, GROUPS)),
         ],
         compiler_params=pltpu.CompilerParams(vmem_limit_bytes=56 * 2**20),

time: 60.2 us -> 59.3 us (0.985)
  Pallas kernels: 59.4 us -> 58.5 us
    pallas_call x1, Pallas kernels: 56.1 us -> 55.4 us  [body(): pl.pallas_call(functools.partial(main_kernel, nb, nz), out_shape=[jax.Sha...]
where the time goes in v5:
time: 59.3 us; the launch traced here: 59.2 us
  Pallas kernels  58.5 us (99%)
  between operations  0.64 us (1%)
    pallas_call x1, Pallas kernels, body(): pl.pallas_call(functools.partial(main_kernel, nb, nz), out_shape=[jax.Sha...  55.4 us
    pallas_call x1, Pallas kernels, body(): pl.pallas_call(functools.partial(unpack_kernel, nj, nz, 1.0 / slots ** 0....  3.1 us

profile of v5, /device:TPU:1, one launch (start us, length us, event | category | flops | bytes accessed | tf_op | source)
XLA Modules:
  0.0 59.2 jit_solution(6979337840750586064)
XLA Ops:
  0.6 55.4 %halo_conv_and_sum.1 = (bf16[96,256]{1,0:T(8,128)(2,1)}, bf16[96,256]{1,0:T(8,128)(2,1)}, bf16[2,16,2,64,128]{4,3,2,1,0:T(8,128)(2,1)}) custom-call(bf16[1,96,256]{2,1,0:T(8,128)(2,1)} %feat_in.1, s32[1,256]{1,0:T(1,128)} %act_in.1, s32[27,1,256]{2,1,0:T(1,128)} %bitcast.3, s32[1,1,8,32]{3,2,1,0:T(8,128)} %lists_in.1, bf16[27,96,96]{2,1,0:T(8,128)(2,1)} %w1_in.1, ...), custom_call_target="tpu_custom_call" | custom-call | tf_op jit(solution)/shard_map/halo_conv_and_sum/pallas_call | solution.py:575
  56.1 3.1 %unpack.1 = (f32[27,96,96]{2,1,0:T(8,128)}, f32[27,96,96]{2,1,0:T(8,128)}, bf16[1,96,256]{2,1,0:T(8,128)(2,1)}, bf16[1,96,256]{2,1,0:T(8,128)(2,1)}) custom-call(bf16[96,256]{1,0:T(8,128)(2,1)} %get-tuple-element.11.field_in, bf16[96,256]{1,0:T(8,128)(2,1)} %get-tuple-element.12.grad_in, bf16[2,2048,128]{2,1,0:T(8,128)(2,1)} %bitcast.2), custom_call_target="tpu_custom_call" | custom-call | tf_op jit(solution)/shard_map/unpack/pallas_call | solution.py:629

commit v6 on v5

--- a/solution.py
+++ b/solution.py
@@ -16,6 +16,7 @@
 GROUPS = 7
 CORNER = 16
 UNROLL = 9
+FIRST_UNROLL = 9
 
 
 def nn(a, b):
@@ -49,7 +50,7 @@
     feat, act, nbr, lists, w1, w2, cot, results, spreading,
     field, pick, sent_a, halo_a, sent_c, halo_c,
     local_hot, halo_hot, turned, side_by_side, picked, sides,
-    to_core, own, from_core, summed, arrived, z_part, z_in, z_out,
+    to_core, own, from_core, summed, arrived, z_part, z_send, z_in, z_out,
     heard, sem_in, sem_out, sem_a, sem_c, sem_core, sem_plane, sem_z, sem_zg, sem_gather, sem_keep, sem_forward,
 ):
     bf16, f32 = jnp.bfloat16, jnp.float32
@@ -60,7 +61,8 @@
     nj = nb // 2
     half_rows = own.shape[0]
     piece = half_rows // nj
-    sliver = piece // nz
+    owners = nz // 2
+    sliver = piece // owners
     quarter = piece // 4
     some = piece // 2
     group_rows = GROUP * channels * channels // 128
@@ -252,15 +254,15 @@
     zeros = jnp.zeros((channels, voxels), f32)
 
     def first_pass(step, _):
-        for u in range(UNROLL):
-            o = step * UNROLL + u
+        for u in range(FIRST_UNROLL):
+            o = step * FIRST_UNROLL + u
             mirror = OFFSETS - 1 - o
             got = nn(turned_halo, halo_hot[o]).astype(bf16)
             picked[0, at(o), :] += got[:channels]
             picked[1, at(mirror), :] += got[channels:]
         return 0
 
-    lax.fori_loop(0, OFFSETS // UNROLL, first_pass, 0)
+    lax.fori_loop(0, OFFSETS // FIRST_UNROLL, first_pass, 0)
     hear_plane(1)
     hear_samples(1)
     tell(2)
@@ -327,7 +329,7 @@
     join()
 
     def quarter_rows(q):
-        return pl.ds(pl.multiple_of(q * quarter, 8), quarter)
+        return pl.ds(pl.multiple_of(q * quarter, 16), quarter)
 
     starts = (far, near)
 
@@ -343,23 +345,27 @@
     for part in range(2):
         loop(0, nj - 1, lambda k: plane_copy(part, chip, plane(k)).start())
 
+    def owner(w):
+        return 2 * w + core
+
+    owns = lax.rem(smp, 2) == core
+    here = lax.div(smp, 2)
+
     def z_copy(source, target, rows):
-        return remote(z_part.at[rows, :], z_in.at[source], sem_z, source, target, (blk, target))
+        return remote(z_send.at[rows, :], z_in.at[source], sem_z, source, target, (blk, target))
+
+    def part_owners(start, act_on):
+        def run(k):
+            w = lax.rem(start * (owners // 4) + k, owners)
+            pl.when(owner(w) != smp)(lambda: act_on(w, k))
+
+        loop(0, owners // 2, run)
 
     def z_sends(part, act_on):
-        def run(k):
-            target = lax.rem(starts[part] * (nz // 4) + k, nz)
-            rows = pl.ds(pl.multiple_of(part * some + k * sliver, 8), sliver)
-
-            if part == 0:
-                act_on(target, rows)
-            else:
-
-                @pl.when(target != smp)
-                def _():
-                    act_on(target, rows)
-
-        loop(0, nz // 2, run)
+        def run(w, k):
+            act_on(owner(w), pl.ds(pl.multiple_of(part * some + k * sliver, 16), sliver))
+
+        part_owners(starts[part], run)
 
     hear_samples(2)
     base = pl.multiple_of(chip * piece, piece)
@@ -376,6 +382,7 @@
             z_part[part * some : (part + 1) * some, :] += arrived[part, source].astype(f32)
 
         loop(0, nj - 1, add_piece)
+        z_send[part * some : (part + 1) * some, :] = z_part[part * some : (part + 1) * some, :].astype(bf16)
         z_sends(part, lambda target, rows: z_copy(smp, target, rows).start())
 
     arrive_faces(faces_c)
@@ -393,27 +400,25 @@
     most = OFFSETS // UNROLL - 1
     forth, back = lax.fori_loop(0, most, second_pass, (zeros, zeros))
 
-    place_here = lax.rem(smp + nz - near * (nz // 4), nz)
-    total = z_part[pl.ds(pl.multiple_of(some + place_here * sliver, 8), sliver), :]
-
-    def add_sliver(i, running):
-        source = along(i)
-        z_copy(source, source, pl.ds(0, sliver)).wait_recv()
-        return running + z_in[source]
-
-    total = lax.fori_loop(1, nz, add_sliver, total)
-
-    def sliver_rows(s):
-        return pl.ds(pl.multiple_of(s * sliver, 8), sliver)
-
-    def zg_copy(source, target):
-        return remote(
-            z_out.at[sliver_rows(source), :], z_out.at[sliver_rows(source), :], sem_zg, source, target,
-            (blk, target),
-        )
-
-    z_out[sliver_rows(smp), :] = total
-    loop(0, nz - 1, lambda k: zg_copy(smp, along(ring_step(k, nz))).start())
+    def sliver_rows(w):
+        return pl.ds(pl.multiple_of(w * sliver, 16), sliver)
+
+    def zg_copy(w, target):
+        part = z_out.at[sliver_rows(w), :]
+        return remote(part, part, sem_zg, owner(w), target, (blk, target))
+
+    @pl.when(owns)
+    def _():
+        place_here = lax.rem(here + owners - near * (owners // 4), owners)
+
+        def add_sliver(i, running):
+            source = along(i)
+            z_copy(source, source, pl.ds(0, sliver)).wait_recv()
+            return running + z_in[source].astype(f32)
+
+        total = z_part[pl.ds(pl.multiple_of(some + place_here * sliver, 16), sliver), :]
+        z_out[sliver_rows(here), :] = lax.fori_loop(1, nz, add_sliver, total).astype(bf16)
+        loop(0, nz - 1, lambda k: zg_copy(here, along(ring_step(k, nz))).start())
 
     forth, back = lax.fori_loop(most, OFFSETS // UNROLL, second_pass, (forth, back))
     results[0] = (live_f * forth).astype(bf16)
@@ -454,22 +459,19 @@
 
     for part, start in enumerate((near, far)):
 
-        def sliver_here(k):
-            source = lax.rem(start * (nz // 4) + k, nz)
-            if part == 0:
-                pl.when(source != smp)(lambda: zg_copy(source, source).wait_recv())
-            else:
-                zg_copy(source, source).wait_recv()
-
-        loop(0, nz // 2, sliver_here)
+        part_owners(start, lambda w, k: zg_copy(w, smp).wait_recv())
         for k in range(2):
             spreading[chip, part, k * quarter : (k + 1) * quarter, :] = z_out[
                 quarter_rows(lax.rem(start + k, 4)), :
-            ].astype(bf16)
+            ]
         loop(0, nj - 1, lambda k: gather_copy(part, chip, plane(k)).start())
         store(part, chip)
 
-    loop(1, nz, lambda i: zg_copy(smp, along(i)).wait_send())
+
+    @pl.when(owns)
+    def _():
+        loop(1, nz, lambda i: zg_copy(here, along(i)).wait_send())
+
     for copy in keeps:
         copy.wait()
     for part in range(2):
@@ -603,8 +605,9 @@
             pltpu.VMEM((nj, piece + piece // 4, 128), bf16),
             pltpu.VMEM((2, nj, piece // 2, 128), bf16),
             pltpu.VMEM((piece, 128), f32),
-            pltpu.VMEM((nz, piece // nz, 128), f32),
-            pltpu.VMEM((piece, 128), f32),
+            pltpu.VMEM((piece, 128), bf16),
+            pltpu.VMEM((nz, piece // (nz // 2), 128), bf16),
+            pltpu.VMEM((piece, 128), bf16),
             pltpu.SemaphoreType.REGULAR((2, 3)),
             dma((7,)),
             dma((2,)),

time: 59.3 us -> 59.4 us (level)
  no operation moved by 1% of the time
where the time goes in v6:
time: 59.4 us; the launch traced here: 59.2 us
  Pallas kernels  58.6 us (99%)
  between operations  0.64 us (1%)
    pallas_call x1, Pallas kernels, body(): pl.pallas_call(functools.partial(main_kernel, nb, nz), out_shape=[jax.Sha...  55.5 us
    pallas_call x1, Pallas kernels, body(): pl.pallas_call(functools.partial(unpack_kernel, nj, nz, 1.0 / slots ** 0....  3.1 us

profile of v6, /device:TPU:1, one launch (start us, length us, event | category | flops | bytes accessed | tf_op | source)
XLA Modules:
  0.0 59.2 jit_solution(9381297985486266557)
XLA Ops:
  0.6 55.5 %halo_conv_and_sum.1 = (bf16[96,256]{1,0:T(8,128)(2,1)}, bf16[96,256]{1,0:T(8,128)(2,1)}, bf16[2,16,2,64,128]{4,3,2,1,0:T(8,128)(2,1)}) custom-call(bf16[1,96,256]{2,1,0:T(8,128)(2,1)} %feat_in.1, s32[1,256]{1,0:T(1,128)} %act_in.1, s32[27,1,256]{2,1,0:T(1,128)} %bitcast.3, s32[1,1,8,32]{3,2,1,0:T(8,128)} %lists_in.1, bf16[27,96,96]{2,1,0:T(8,128)(2,1)} %w1_in.1, ...), custom_call_target="tpu_custom_call" | custom-call | tf_op jit(solution)/shard_map/halo_conv_and_sum/pallas_call | solution.py:577
  56.1 3.1 %unpack.1 = (f32[27,96,96]{2,1,0:T(8,128)}, f32[27,96,96]{2,1,0:T(8,128)}, bf16[1,96,256]{2,1,0:T(8,128)(2,1)}, bf16[1,96,256]{2,1,0:T(8,128)(2,1)}) custom-call(bf16[96,256]{1,0:T(8,128)(2,1)} %get-tuple-element.11.field_in, bf16[96,256]{1,0:T(8,128)(2,1)} %get-tuple-element.12.grad_in, bf16[2,2048,128]{2,1,0:T(8,128)(2,1)} %bitcast.2), custom_call_target="tpu_custom_call" | custom-call | tf_op jit(solution)/shard_map/unpack/pallas_call | solution.py:632

commit v7 on v6

--- a/solution.py
+++ b/solution.py
@@ -16,7 +16,8 @@
 GROUPS = 7
 CORNER = 16
 UNROLL = 9
-FIRST_UNROLL = 9
+FIRST_UNROLL = 27
+CHUNKS = ((0, 7),)
 
 
 def nn(a, b):
@@ -284,26 +285,31 @@
         rows = pl.ds(pl.multiple_of(g * group_rows, 32), group_rows)
         return remote(to_core.at[rows, :], from_core.at[rows, :], sem_core, g, g, partner)
 
-    def correlate(which, g):
-        rows = pl.ds(pl.multiple_of(g * (GROUP * channels), 128), GROUP * channels)
+    def correlate(which, groups, dtype):
+        wide = GROUP * channels
+        rows = pl.ds(groups[0] * wide, (groups[1] - groups[0]) * wide)
         if which == 0:
-            return nt(sides[0], picked[0, rows, :])
-        tall = nt(picked[1, rows, :], sides[1])
-        return jnp.concatenate([tall[k * channels : (k + 1) * channels] for k in range(GROUP)], axis=1)
-
-    def tile_rows(g, t):
-        return pl.ds(pl.multiple_of(g * group_rows + t * channels, 32), channels)
-
-    def give(which, g):
-        product = correlate(which, g)
+            flat = nt(sides[0], picked[0, rows, :]).astype(dtype)
+            return [flat[:, n * wide : (n + 1) * wide] for n in range(groups[1] - groups[0])]
+        tall = nt(picked[1, rows, :], sides[1]).astype(dtype)
+        return [
+            jnp.concatenate([tall[n + k * channels : n + (k + 1) * channels] for k in range(GROUP)], axis=1)
+            for n in range(0, tall.shape[0], wide)
+        ]
+
+    def put(where, g, block):
         for t in range(tiles):
-            to_core[tile_rows(g, t), :] = product[:, t * 128 : (t + 1) * 128].astype(bf16)
-        core_copy(g).start()
-
-    def keep(which, g):
-        product = correlate(which, g)
-        for t in range(tiles):
-            own[tile_rows(g, t), :] = product[:, t * 128 : (t + 1) * 128]
+            rows = pl.ds(g * group_rows + t * channels, channels)
+            where[rows, :] = block[:, t * 128 : (t + 1) * 128]
+
+    def give(which, groups):
+        for g, block in zip(range(*groups), correlate(which, groups, bf16)):
+            put(to_core, g, block)
+            core_copy(g).start()
+
+    def keep(which, groups):
+        for g, block in zip(range(*groups), correlate(which, groups, f32)):
+            put(own, g, block)
 
     def join():
         done = 0
@@ -321,10 +327,10 @@
 
         @pl.when(core == which)
         def _():
-            for g in range(GROUPS):
-                give(1 - which, g)
-            for g in range(GROUPS):
-                keep(which, g)
+            for groups in CHUNKS:
+                give(1 - which, groups)
+            for groups in CHUNKS:
+                keep(which, groups)
 
     join()
 

time: 59.4 us -> 57.7 us (0.971)
  Pallas kernels: 58.6 us -> 57 us
    pallas_call x1, Pallas kernels: 55.5 us -> 53.9 us  [body(): pl.pallas_call(functools.partial(main_kernel, nb, nz), out_shape=[jax.Sha...]
where the time goes in v7:
time: 57.7 us; the launch traced here: 57.6 us
  Pallas kernels  57 us (99%)
  between operations  0.64 us (1%)
    pallas_call x1, Pallas kernels, body(): pl.pallas_call(functools.partial(main_kernel, nb, nz), out_shape=[jax.Sha...  53.9 us
    pallas_call x1, Pallas kernels, body(): pl.pallas_call(functools.partial(unpack_kernel, nj, nz, 1.0 / slots ** 0....  3.1 us

profile of v7, /device:TPU:1, one launch (start us, length us, event | category | flops | bytes accessed | tf_op | source)
XLA Modules:
  0.0 57.6 jit_solution(926092477093790078)
XLA Ops:
  0.6 53.9 %halo_conv_and_sum.1 = (bf16[96,256]{1,0:T(8,128)(2,1)}, bf16[96,256]{1,0:T(8,128)(2,1)}, bf16[2,16,2,64,128]{4,3,2,1,0:T(8,128)(2,1)}) custom-call(bf16[1,96,256]{2,1,0:T(8,128)(2,1)} %feat_in.1, s32[1,256]{1,0:T(1,128)} %act_in.1, s32[27,1,256]{2,1,0:T(1,128)} %bitcast.3, s32[1,1,8,32]{3,2,1,0:T(8,128)} %lists_in.1, bf16[27,96,96]{2,1,0:T(8,128)(2,1)} %w1_in.1, ...), custom_call_target="tpu_custom_call" | custom-call | tf_op jit(solution)/shard_map/halo_conv_and_sum/pallas_call | solution.py:583
  54.5 3.1 %unpack.1 = (f32[27,96,96]{2,1,0:T(8,128)}, f32[27,96,96]{2,1,0:T(8,128)}, bf16[1,96,256]{2,1,0:T(8,128)(2,1)}, bf16[1,96,256]{2,1,0:T(8,128)(2,1)}) custom-call(bf16[96,256]{1,0:T(8,128)(2,1)} %get-tuple-element.11.field_in, bf16[96,256]{1,0:T(8,128)(2,1)} %get-tuple-element.12.grad_in, bf16[2,2048,128]{2,1,0:T(8,128)(2,1)} %bitcast.2), custom_call_target="tpu_custom_call" | custom-call | tf_op jit(solution)/shard_map/unpack/pallas_call | solution.py:638

commit v8 on v7

--- a/solution.py
+++ b/solution.py
@@ -449,8 +449,8 @@
             device_id=(target * 2 + core, smp), device_id_type=MESH,
         )
 
-    def keep_copy(part, p):
-        return pltpu.make_async_copy(spreading.at[p, part], gathered.at[core, p, part], sem_keep.at[part])
+    def keep_copy(part):
+        return pltpu.make_async_copy(spreading.at[:, part], gathered.at[core, :, part], sem_keep.at[part])
 
     def forward_copy(which, part, p):
         return pltpu.make_async_remote_copy(
@@ -460,7 +460,6 @@
         )
 
     def store(part, p):
-        keep_copy(part, p).start()
         forward_copy(core, part, p).start()
 
     for part, start in enumerate((near, far)):
@@ -488,9 +487,10 @@
             store(part, source)
 
         loop(0, nj - 1, hand_on)
+        keep_copy(part).start()
         loop(0, nj - 1, lambda k: gather_copy(part, chip, plane(k)).wait_send())
     for part in range(2):
-        pltpu.make_async_copy(spreading.at[:, part], gathered.at[core, :, part], sem_keep.at[part]).wait()
+        keep_copy(part).wait()
         forwarded = pltpu.make_async_remote_copy(
             src_ref=spreading.at[:, part], dst_ref=gathered.at[other, :, part],
             send_sem=sem_forward.at[0, part], recv_sem=sem_forward.at[1, part],

time: 57.7 us -> 57.7 us (level)
  no operation moved by 1% of the time
where the time goes in v8:
time: 57.7 us; the launch traced here: 57.6 us
  Pallas kernels  57 us (99%)
  between operations  0.64 us (1%)
    pallas_call x1, Pallas kernels, body(): pl.pallas_call(functools.partial(main_kernel, nb, nz), out_shape=[jax.Sha...  53.9 us
    pallas_call x1, Pallas kernels, body(): pl.pallas_call(functools.partial(unpack_kernel, nj, nz, 1.0 / slots ** 0....  3.1 us

profile of v8, /device:TPU:1, one launch (start us, length us, event | category | flops | bytes accessed | tf_op | source)
XLA Modules:
  0.0 57.6 jit_solution(12783081485912898261)
XLA Ops:
  0.6 53.9 %halo_conv_and_sum.1 = (bf16[96,256]{1,0:T(8,128)(2,1)}, bf16[96,256]{1,0:T(8,128)(2,1)}, bf16[2,16,2,64,128]{4,3,2,1,0:T(8,128)(2,1)}) custom-call(bf16[1,96,256]{2,1,0:T(8,128)(2,1)} %feat_in.1, s32[1,256]{1,0:T(1,128)} %act_in.1, s32[27,1,256]{2,1,0:T(1,128)} %bitcast.3, s32[1,1,8,32]{3,2,1,0:T(8,128)} %lists_in.1, bf16[27,96,96]{2,1,0:T(8,128)(2,1)} %w1_in.1, ...), custom_call_target="tpu_custom_call" | custom-call | tf_op jit(solution)/shard_map/halo_conv_and_sum/pallas_call | solution.py:583
  54.5 3.1 %unpack.1 = (f32[27,96,96]{2,1,0:T(8,128)}, f32[27,96,96]{2,1,0:T(8,128)}, bf16[1,96,256]{2,1,0:T(8,128)(2,1)}, bf16[1,96,256]{2,1,0:T(8,128)(2,1)}) custom-call(bf16[96,256]{1,0:T(8,128)(2,1)} %get-tuple-element.11.field_in, bf16[96,256]{1,0:T(8,128)(2,1)} %get-tuple-element.12.grad_in, bf16[2,2048,128]{2,1,0:T(8,128)(2,1)} %bitcast.2), custom_call_target="tpu_custom_call" | custom-call | tf_op jit(solution)/shard_map/unpack/pallas_call | solution.py:638
